TPU v7x, 32 devices: a whole 2x2x4 slice. The times are simulated.
32 devices in a mesh: segment: 2 (over core), dp: 8 (over z, y), tensor: 2 (over x).
Axes of the slice: x: 2, y: 2, z: 4, core: 2. Of those that a mesh axis runs over, the one named last changes fastest.
Arguments:
- layer_input: bfloat16 [2, 8, 128, 768], P(None, 'dp'), may hold values from -8 to 8
- doc_lengths: int32 [2, 8, 3], P(None, 'dp'), may hold values from 1 to 4, 8 in all within a row
- norm_gains: float32 [2, 2, 768], P('segment'), may hold values from 0.5 to 1.5
- mixing: bfloat16 [2, 768, 4, 768], P('segment', None, None, 'tensor'), may hold values from -0.21875 to 0.21875
- rate_weight: bfloat16 [2, 768, 12], P('segment', None, 'tensor'), may hold values from -0.21875 to 0.21875
- rate_offset: float32 [2, 12], P('segment', 'tensor'), may hold values from -1 to 1
- expand: float32 [2, 12, 64, 256], P('segment', 'tensor'), may hold values from -0.75 to 0.75
- hidden_bias: float32 [2, 12, 256], P('segment', 'tensor'), may hold values from -3 to 3
- contract: float32 [2, 12, 256, 64], P('segment', 'tensor'), may hold values from -0.375 to 0.375
- result_bias: float32 [2, 12, 64], P('segment', 'tensor'), may hold values from -3 to 3
- head_gains: float32 [2, 2, 12, 64], P('segment', None, 'tensor'), may hold values from 0.5 to 1.5
- head_shift: float32 [2, 12, 64], P('segment', 'tensor'), may hold values from -2 to 2
- output_proj: bfloat16 [2, 768, 768], P('segment', 'tensor'), may hold values from -0.4375 to 0.4375
- swiglu: bfloat16 [2, 768, 2, 2048], P('segment', None, None, 'tensor'), may hold values from -0.21875 to 0.21875
- down_proj: bfloat16 [2, 2048, 768], P('segment', 'tensor'), may hold values from -0.25 to 0.25
- cotangent: bfloat16 [2, 8, 128, 768], P(None, 'dp'), may hold values from -6 to 6
Outputs:
- layer_output: bfloat16 [2, 2, 8, 128, 768], P('segment', None, 'dp')
- input_grads: float32 [2, 2, 8, 128, 768], P('segment', None, 'dp')
- grad_gains: float32 [2, 2, 768], P('segment')
- grad_mixing: float32 [2, 768, 4, 768], P('segment', None, None, 'tensor')
- grad_rate: float32 [2, 768, 12], P('segment', None, 'tensor')
- grad_offset: float32 [2, 12], P('segment', 'tensor')
- grad_expand: float32 [2, 12, 64, 256], P('segment', 'tensor')
- grad_hidden: float32 [2, 12, 256], P('segment', 'tensor')
- grad_contract: float32 [2, 12, 256, 64], P('segment', 'tensor')
- grad_result: float32 [2, 12, 64], P('segment', 'tensor')
- grad_heads: float32 [2, 2, 12, 64], P('segment', None, 'tensor')
- grad_shift: float32 [2, 12, 64], P('segment', 'tensor')
- grad_output: float32 [2, 768, 768], P('segment', 'tensor')
- grad_swiglu: float32 [2, 768, 2, 2048], P('segment', None, None, 'tensor')
- grad_down: float32 [2, 2048, 768], P('segment', 'tensor')
- rate_stats: float32 [2, 2, 8, 2, 12], P('segment')
Inputs may be any that keep to these rules, and one draw needn't show every extreme that they name: `doc_lengths`: lengths are counted in inner blocks of 16 tokens; the 3 lengths of a row sum to 8, and in every row the longest is exactly 4.
All inputs are finite; a program needn't handle non-finite values.
Results may differ from a plain program's by a relative error of at most 0.023.
Values may be sent and summed in bfloat16 or wider, within the bound.
No kernel may reach another device: no remote copies, remote signals or barrier semaphores. Data moves between devices by JAX's collectives and lax.ppermute only.
A program may use at most 192 MiB of HBM per device.

v0:
```python
import functools
import jax
import jax.numpy as jnp
from jax import lax
from jax.experimental import pallas as pl
from jax.experimental.pallas import tpu as pltpu
from jax.sharding import PartitionSpec as P

MBT = 16
EPS = 1e-06
RATE = 0.125
C0 = 0.7978845608028654
BF = jnp.bfloat16
F32 = jnp.float32
VMEM = pl.BlockSpec(memory_space=pltpu.VMEM)
SMEM = pl.BlockSpec(memory_space=pltpu.SMEM)
HBM = pl.BlockSpec(memory_space=pltpu.HBM)
LOAD = "load"
NRM, INV, MIS, MEANN, GZ2 = range(5)
NA, INVA, NO, INVO, GATE = range(5)
RATE_ROW, HIDDEN_ROW, HEAD_ROW, OFFSET_ROW, GAIN_ROW, STAT_ROW = 0, 18, 24, 30, 31, 40
PACK_ROWS = 1152


def dot(a, b):
    return jnp.dot(a, b, preferred_element_type=F32)


def dot_t(a, b):
    return lax.dot_general(a, b, (((1,), (1,)), ((), ())), preferred_element_type=F32)


def tdot(a, b):
    return lax.dot_general(a, b, (((0,), (0,)), ((), ())), preferred_element_type=F32)


def cat(parts, axis):
    return jnp.concatenate(parts, axis=axis)


def gelu_parts(z):
    z2 = z * z
    t = jnp.tanh(C0 * z * (1.0 + 0.044715 * z2))
    h = 0.5 * (1.0 + t)
    du = C0 * (1.0 + 0.134145 * z2)
    sech = 1.0 - t * t
    value = z * h
    slope = h + 0.5 * z * sech * du
    return value, slope, t, z2, du, sech


def gelu_two(z):
    value, slope, _, _, _, _ = gelu_parts(z)
    return value, slope


def gelu_curve(z):
    _, _, t, z2, du, sech = gelu_parts(z)
    return sech * (C0 * (1.0 + 0.26829 * z2) - z * t * du * du)


def rms_inv(values):
    return lax.rsqrt(jnp.mean(values * values, axis=-1, keepdims=True) + EPS)


class Pick:
    def __init__(self, layer, sems):
        self.own = lax.axis_index("segment") == layer
        self.sems = sems
        self.count = 0

    def start(self, own_ref, other_ref, dst):
        sem = self.sems.at[self.count]
        self.count += 1

        @pl.when(self.own)
        def _():
            pltpu.make_async_copy(own_ref, dst, sem).start()

        @pl.when(jnp.logical_not(self.own))
        def _():
            pltpu.make_async_copy(other_ref, dst, sem).start()

        return pltpu.make_async_copy(own_ref, dst, sem)


def doc_places(dl_ref, steps):
    core = lax.axis_index("segment")
    one, two = dl_ref[core, 0], dl_ref[core, 1]
    begin = jnp.where(one == steps, 0, jnp.where(two == steps, one, one + two))
    cut = jnp.where(one == steps, two, one)
    return begin, cut


def block_starts(begin, steps):
    places = []
    for s in range(steps):
        places.append(pl.multiple_of((begin + s) * MBT, MBT))
        places.append(pl.multiple_of(jnp.where(s < begin, s, s + steps) * MBT, MBT))
    return places


def gather_rows(ref, lead, places):
    return cat([ref[lead, pl.ds(p, MBT), :] for p in places], 0)


def scatter_rows(ref, places, value):
    for i, p in enumerate(places):
        ref[pl.ds(p, MBT), :] = value[i * MBT : (i + 1) * MBT, :]


def turned_mask(cut, length):
    i = lax.broadcasted_iota(jnp.int32, (length, length), 0)
    j = lax.broadcasted_iota(jnp.int32, (length, length), 1)
    si, li, sj, lj = i >> 5, (i >> 4) & 1, length // 32 - 1 - (j >> 5), (j >> 4) & 1
    di = jnp.where(li == 0, 0, jnp.where(si < cut, 1, 2))
    dj = jnp.where(lj == 0, 0, jnp.where(sj < cut, 1, 2))
    return jnp.where((di == dj) & (si < sj), 1.0 / MBT, 0.0)


def masks(cut, length):
    def parts(axis):
        i = lax.broadcasted_iota(jnp.int32, (length, length), axis)
        step, lane, t = i >> 5, (i >> 4) & 1, i & 15
        doc = jnp.where(lane == 0, 0, jnp.where(step < cut, 1, 2))
        return step, lane, t, doc

    s0, l0, t0, d0 = parts(0)
    s1, l1, t1, d1 = parts(1)
    same = d0 == d1
    block = (s0 == s1) & (l0 == l1)
    past = jnp.where(same & (s1 < s0), 1.0 / MBT, 0.0)
    past_t = jnp.where(same & (s0 < s1), 1.0 / MBT, 0.0)
    inside = jnp.where(block & (t1 <= t0), 1.0 / (t0 + 1).astype(F32), 0.0)
    inside_t = jnp.where(block & (t0 <= t1), 1.0 / (t1 + 1).astype(F32), 0.0)
    return past, past + inside, past_t, past_t + inside_t


class Halves:
    def __init__(self):
        lane = lax.broadcasted_iota(jnp.int32, (1, 128), 1)
        self.left = lane < 64
        r = lax.broadcasted_iota(jnp.int32, (256, 128), 0) & 127
        c = lax.broadcasted_iota(jnp.int32, (256, 128), 1)
        self.mean_mat = jnp.where((r < 64) == (c < 64), 1.0 / 64.0, 0.0).astype(BF)

    def mean(self, x):
        high = x.astype(BF)
        low = (x - high.astype(F32)).astype(BF)
        return dot(cat([high, low], 1), self.mean_mat)

    def split(self, x):
        zero = jnp.zeros_like(x)
        return cat([jnp.where(self.left, x, zero), jnp.where(self.left, zero, x)], 0)

    def pack(self, a, b):
        return jnp.where(self.left, a, b)

    def both(self, weights, values):
        rows = weights[0].shape[0]
        full = dot(cat(weights, 0), values)
        return self.pack(full[:rows], full[rows:])


def pair_weights(inner_ref, small_ref, heads, p, halves):
    width = inner_ref.shape[2]
    zero = jnp.zeros((64, width), BF)

    def blocks(a, b):
        return cat([cat([a, zero], 1), cat([zero, b], 1)], 0)

    def centred(index):
        w = inner_ref[heads + index].astype(F32)
        return (w - jnp.mean(w, axis=0, keepdims=True)).astype(BF)

    w1 = blocks(inner_ref[2 * p], inner_ref[2 * p + 1])
    w2 = blocks(centred(2 * p), centred(2 * p + 1))
    return w1, w2


def join(parts):
    return cat(parts, 0) if len(parts) > 1 else parts[0]


def pad_rows(parts, rows):
    have = sum(x.shape[0] for x in parts)
    if have < rows:
        parts = parts + [jnp.zeros((rows - have, parts[0].shape[1]), parts[0].dtype)]
    return cat(parts, 0) if len(parts) > 1 else parts[0]


def mixer_unrolled(refs, x_one, mix_ref, rate_ref, inner_ref, small_ref, begin_cut, x1_ready):
    (mixed_ref, stats_ref, kq_ref, x2_ref, g1_ref, y2_ref, d1_ref, ud2_ref, e1_ref, sm_ref, so_ref, sg_ref) = refs
    _, cut = begin_cut
    length = x_one.shape[0]
    heads = inner_ref.shape[0] // 2
    pairs = heads // 2
    hid = inner_ref.shape[2]
    wide = heads * 64
    steps = length // (2 * MBT)
    rows = 2 * MBT
    past, near, _, _ = masks(cut, length)
    hv = Halves()
    proj = dot(x_one, mix_ref[...])
    logits = dot_t(x_one, rate_ref[...]) + small_ref[3:4, 0:16]
    sg = jax.nn.sigmoid(logits)
    sg_ref[...] = sg
    stats_ref[...] = cat(
        [jnp.mean(sg, axis=0, keepdims=True), jnp.max(sg, axis=0, keepdims=True)], 0
    )
    rates = RATE * sg
    st = []
    for p in range(pairs):
        c = slice(128 * p, 128 * p + 128)
        h = slice(2 * hid * p, 2 * hid * (p + 1))
        q, k, v, gate = [proj[:, wide * i + 128 * p : wide * i + 128 * p + 128] for i in range(4)]
        d = dict(q=q, gate=gate, diff=v - k, c=c, h=h)
        d["w1"], d["w2"] = pair_weights(inner_ref, small_ref, heads, p, hv)
        d["b1"] = small_ref[0:1, h]
        b2 = small_ref[2:3, 128 * p : 128 * p + 128]
        d["b2"] = b2 - hv.mean(jnp.broadcast_to(b2, (8, 128)))[0:1]
        d["g"] = small_ref[2:3, wide + 128 * p : wide + 128 * p + 128]
        d["gp"] = small_ref[2:3, 2 * wide + 128 * p : 2 * wide + 128 * p + 128]
        d["be"] = small_ref[2:3, 3 * wide + 128 * p : 3 * wide + 128 * p + 128]
        d["r"] = [rates[:, 2 * p + i : 2 * p + i + 1] for i in range(2)]
        d["rp"] = hv.pack(d["r"][0], d["r"][1])
        d["kb"], d["qb"] = k.astype(BF), q.astype(BF)
        kq_ref[:, c] = d["kb"]
        kq_ref[:, wide + 128 * p : wide + 128 * p + 128] = d["qb"]
        d["base"] = dot(d["kb"], d["w1"]) + d["b1"]
        kk = dot_t(hv.split(d["kb"]), d["kb"])
        d["m1"] = [(past * (kk[i * length : (i + 1) * length] + 1.0)).astype(BF) for i in range(2)]
        for name in ("x2", "g1", "g2", "z1", "u"):
            d[name] = []
        st.append(d)
    kq_ref.send()
    sg_ref.send()
    for s in range(steps):
        sl = slice(rows * s, rows * s + rows)
        for p in range(pairs):
            d = st[p]
            c, h = d["c"], d["h"]
            z1 = d["base"][sl]
            if s:
                g1 = pad_rows(d["g1"], length)
                x2 = pad_rows(d["x2"], length)
                g2 = pad_rows(d["g2"], length)
                z1 = z1 - cat([dot(d["m1"][i][sl], g1[:, hid * i : hid * (i + 1)]) for i in range(2)], 1)
            act, slope = gelu_two(z1)
            actb = act.astype(BF)
            z2 = dot_t(actb, d["w2"]) + d["b2"]
            if s:
                far = [
                    (past[sl] * (dot_t(actb[:, hid * i : hid * (i + 1)], x2[:, hid * i : hid * (i + 1)]) + 1.0)).astype(BF)
                    for i in range(2)
                ]
                z2 = z2 - dot(cat(far, 1), hv.split(g2))
            inv = lax.rsqrt(hv.mean(z2 * z2) + EPS)
            n = z2 * inv
            mis = n * d["g"] + d["be"] - d["diff"][sl]
            misg = mis * d["g"]
            both = hv.mean(cat([misg, misg * n], 0))
            gz2 = (misg - both[:rows] - n * both[rows:]) * inv
            gz2b = gz2.astype(BF)
            u = dot(gz2b, d["w2"])
            if s:
                f = dot_t(hv.split(gz2b), g2)
                u = u - cat(
                    [
                        dot((past[sl] * f[rows * i : rows * (i + 1)]).astype(BF), x2[:, hid * i : hid * (i + 1)])
                        for i in range(2)
                    ],
                    1,
                )
            gz1 = u * slope
            r0, r1 = d["r"][0][sl], d["r"][1][sl]
            g1n = cat([gz1[:, :hid] * r0, gz1[:, hid:] * r1], 1).astype(BF)
            g2n = (gz2 * d["rp"][sl]).astype(BF)
            d["x2"].append(actb)
            d["g1"].append(g1n)
            d["g2"].append(g2n)
            d["z1"].append(z1)
            d["u"].append(u)
            x2_ref[sl, h] = actb
            g1_ref[sl, h] = g1n
            d1_ref[sl, h] = slope.astype(BF)
            sm_ref[NRM, sl, c] = n
            sm_ref[INV, sl, c] = inv
            sm_ref[MIS, sl, c] = mis
            sm_ref[MEANN, sl, c] = both[rows:]
            sm_ref[GZ2, sl, c] = gz2
    for ref in (x2_ref, g1_ref, d1_ref, sm_ref):
        ref.send()
    mixed = []
    for p in range(pairs):
        d = st[p]
        c, h = d["c"], d["h"]
        g1, x2, g2 = cat(d["g1"], 0), cat(d["x2"], 0), cat(d["g2"], 0)
        ud2_ref[:, h] = (cat(d["u"], 0) * gelu_curve(cat(d["z1"], 0))).astype(BF)
        qk = dot_t(hv.split(d["qb"]), d["kb"])
        corr = [
            dot((near * (qk[length * i : length * (i + 1)] + 1.0)).astype(BF), g1[:, hid * i : hid * (i + 1)])
            for i in range(2)
        ]
        act, slope = gelu_two(dot(d["qb"], d["w1"]) + d["b1"] - cat(corr, 1))
        actb = act.astype(BF)
        y2_ref[:, h] = actb
        e1_ref[:, h] = slope.astype(BF)
        far = [
            (near * (dot_t(actb[:, hid * i : hid * (i + 1)], x2[:, hid * i : hid * (i + 1)]) + 1.0)).astype(BF)
            for i in range(2)
        ]
        a2 = dot_t(actb, d["w2"]) + d["b2"] - dot(cat(far, 1), hv.split(g2))
        inv_a = lax.rsqrt(hv.mean(a2 * a2) + EPS)
        n_a = a2 * inv_a
        out = d["q"] + n_a * d["g"] + d["be"]
        inv_o = lax.rsqrt(hv.mean(out * out) + EPS)
        n_o = out * inv_o
        gated, _ = gelu_two(d["gate"])
        low = (gated * n_o * d["gp"]).astype(BF)
        mixed_ref[:, c] = low
        mixed.append(low)
        so_ref[NA, :, c] = n_a
        so_ref[INVA, :, c] = inv_a
        so_ref[NO, :, c] = n_o
        so_ref[INVO, :, c] = inv_o
        so_ref[GATE, :, c] = d["gate"]
    return cat(mixed, 1)


def mixer_forward(refs, x_one, mix_ref, rate_ref, inner_ref, small_ref, begin_cut, work):
    (mixed_ref, stats_ref, kq_ref, x2_ref, g1_ref, y2_ref, d1_ref, ud2_ref, e1_ref, sm_ref, so_ref, sg_ref) = refs
    base_ref, z1_ref, u_ref, m1_ref, g2_ref, w2_ref, past_ref, diff_ref, b2_ref = work
    x2_buf, g1_buf = x2_ref.buf, g1_ref.buf
    _, cut = begin_cut
    length = x_one.shape[0]
    heads = inner_ref.shape[0] // 2
    pairs = heads // 2
    hid = inner_ref.shape[2]
    wide = heads * 64
    steps = length // (2 * MBT)
    rows = 2 * MBT
    past, near, _, _ = masks(cut, length)
    past_ref[...] = past
    hv = Halves()
    proj = dot(x_one, mix_ref[...])
    logits = dot_t(x_one, rate_ref[...]) + small_ref[3:4, 0:16]
    sg = jax.nn.sigmoid(logits)
    sg_ref[...] = sg
    stats_ref[...] = cat(
        [jnp.mean(sg, axis=0, keepdims=True), jnp.max(sg, axis=0, keepdims=True)], 0
    )
    x2_buf[...] = jnp.zeros(x2_buf.shape, BF)
    g1_buf[...] = jnp.zeros(g1_buf.shape, BF)
    g2_ref[...] = jnp.zeros(g2_ref.shape, BF)

    def lanes(p):
        return slice(128 * p, 128 * p + 128), slice(2 * hid * p, 2 * hid * (p + 1))

    def row_of(k, p):
        return small_ref[2:3, wide * k + 128 * p : wide * k + 128 * p + 128]

    firsts = []
    for p in range(pairs):
        c, h = lanes(p)
        q, k, v, gate = [proj[:, wide * i + 128 * p : wide * i + 128 * p + 128] for i in range(4)]
        w1, w2_ref[p] = pair_weights(inner_ref, small_ref, heads, p, hv)
        b2 = row_of(0, p)
        b2_ref[0:1, c] = b2 - hv.mean(jnp.broadcast_to(b2, (8, 128)))[0:1]
        kb, qb = k.astype(BF), q.astype(BF)
        kq_ref[:, c] = kb
        kq_ref[:, wide + 128 * p : wide + 128 * p + 128] = qb
        diff_ref[:, c] = v - k
        so_ref[GATE, :, c] = gate
        base_ref[:, h] = dot(kb, w1) + small_ref[0:1, h]
        kk = dot_t(hv.split(kb), kb)
        for i in range(2):
            m1_ref[2 * p + i] = (past * (kk[i * length : (i + 1) * length] + 1.0)).astype(BF)
        firsts.append((q, kb, qb, w1))
    kq_ref.send()
    sg_ref.send()

    def step(s, carry, start=False):
        at = slice(0, rows) if start else pl.ds(pl.multiple_of(s * rows, rows), rows)
        hv = Halves()
        mask = past_ref[at, :]
        rates = RATE * sg_ref.buf[at, :]
        for p in range(pairs):
            c, h = lanes(p)

            def half(i):
                return slice(2 * hid * p + hid * i, 2 * hid * p + hid * (i + 1))

            w2, g2 = w2_ref[p], g2_ref[p]
            g = row_of(1, p)
            z1 = base_ref[at, h]
            if not start:
                z1 = z1 - cat([dot(m1_ref[2 * p + i, at, :], g1_buf[:, half(i)]) for i in range(2)], 1)
            act, slope = gelu_two(z1)
            actb = act.astype(BF)
            z2 = dot_t(actb, w2) + b2_ref[0:1, c]
            if not start:
                far = [
                    (mask * (dot_t(actb[:, hid * i : hid * (i + 1)], x2_buf[:, half(i)]) + 1.0)).astype(BF)
                    for i in range(2)
                ]
                z2 = z2 - hv.both(far, g2)
            inv = lax.rsqrt(hv.mean(z2 * z2) + EPS)
            n = z2 * inv
            mis = n * g + row_of(3, p) - diff_ref[at, c]
            misg = mis * g
            both = hv.mean(cat([misg, misg * n], 0))
            gz2 = (misg - both[:rows] - n * both[rows:]) * inv
            gz2b = gz2.astype(BF)
            u = dot(gz2b, w2)
            if not start:
                f = dot_t(hv.split(gz2b), g2)
                u = u - cat(
                    [dot((mask * f[rows * i : rows * (i + 1)]).astype(BF), x2_buf[:, half(i)]) for i in range(2)], 1
                )
            gz1 = u * slope
            r0, r1 = rates[:, 2 * p : 2 * p + 1], rates[:, 2 * p + 1 : 2 * p + 2]
            x2_buf[at, h] = actb
            g1_buf[at, h] = cat([gz1[:, :hid] * r0, gz1[:, hid:] * r1], 1).astype(BF)
            g2_ref[p, at, :] = (gz2 * hv.pack(r0, r1)).astype(BF)
            z1_ref[at, h] = z1
            u_ref[at, h] = u
            d1_ref[at, h] = slope.astype(BF)
            sm_ref[NRM, at, c] = n
            sm_ref[INV, at, c] = inv
            sm_ref[MIS, at, c] = mis
            sm_ref[MEANN, at, c] = both[rows:]
            sm_ref[GZ2, at, c] = gz2
        return carry

    step(0, 0, True)
    lax.fori_loop(1, steps, step, 0)
    for ref in (x2_ref, g1_ref, d1_ref, sm_ref):
        ref.send()
    mixed = []
    for p in range(pairs):
        c, h = lanes(p)
        q, kb, qb, w1 = firsts[p]
        g1, x2, g2, w2 = g1_buf[:, h], x2_buf[:, h], g2_ref[p], w2_ref[p]
        ud2_ref[:, h] = (u_ref[:, h] * gelu_curve(z1_ref[:, h])).astype(BF)
        qk = dot_t(hv.split(qb), kb)
        corr = [
            dot((near * (qk[length * i : length * (i + 1)] + 1.0)).astype(BF), g1[:, hid * i : hid * (i + 1)])
            for i in range(2)
        ]
        act, slope = gelu_two(dot(qb, w1) + small_ref[0:1, h] - cat(corr, 1))
        actb = act.astype(BF)
        y2_ref[:, h] = actb
        e1_ref[:, h] = slope.astype(BF)
        far = [
            (near * (dot_t(actb[:, hid * i : hid * (i + 1)], x2[:, hid * i : hid * (i + 1)]) + 1.0)).astype(BF)
            for i in range(2)
        ]
        a2 = dot_t(actb, w2) + b2_ref[0:1, c] - hv.both(far, g2)
        inv_a = lax.rsqrt(hv.mean(a2 * a2) + EPS)
        n_a = a2 * inv_a
        out = q + n_a * row_of(1, p) + row_of(3, p)
        inv_o = lax.rsqrt(hv.mean(out * out) + EPS)
        n_o = out * inv_o
        gated, _ = gelu_two(so_ref.buf[GATE, :, c])
        low = (gated * n_o * row_of(2, p)).astype(BF)
        mixed_ref[:, c] = low
        mixed.append(low)
        so_ref[NA, :, c] = n_a
        so_ref[INVA, :, c] = inv_a
        so_ref[NO, :, c] = n_o
        so_ref[INVO, :, c] = inv_o
    return cat(mixed, 1)


def mixer_backward(dmixed, mixed_refs, inner_ref, small_ref, begin_cut, ig_ref, ms_ref):
    (kq_ref, x2_ref, g1_ref, y2_ref, d1_ref, ud2_ref, e1_ref, sm_ref, so_ref, sg_ref) = mixed_refs
    _, cut = begin_cut
    length = dmixed.shape[0]
    heads = inner_ref.shape[0] // 2
    pairs = heads // 2
    hid = inner_ref.shape[2]
    wide = heads * 64
    steps = length // (2 * MBT)
    rows = 2 * MBT
    past, near, past_t, near_t = masks(cut, length)
    hv = Halves()

    def turned(x):
        return cat([x[rows * k : rows * (k + 1)] for k in reversed(range(steps))], 0)

    past_b = turned_mask(cut, length)
    sg = sg_ref[...]
    rates = RATE * sg

    def by_head(fn):
        return [fn(slice(hid * i, hid * (i + 1)), i) for i in range(2)]

    st = []
    for p in range(pairs):
        c = slice(128 * p, 128 * p + 128)
        h = slice(2 * hid * p, 2 * hid * (p + 1))
        d = dict(c=c, h=h)
        d["w1"], d["w2"] = pair_weights(inner_ref, small_ref, heads, p, hv)
        g = small_ref[2:3, wide + 128 * p : wide + 128 * p + 128]
        gp = small_ref[2:3, 2 * wide + 128 * p : 2 * wide + 128 * p + 128]
        d["g"] = g
        d["r"] = [rates[:, 2 * p + i : 2 * p + i + 1] for i in range(2)]
        d["rp"] = hv.pack(d["r"][0], d["r"][1])
        kb = kq_ref[:, c]
        qb = kq_ref[:, wide + 128 * p : wide + 128 * p + 128]
        x2, g1, y2 = x2_ref[:, h], g1_ref[:, h], y2_ref[:, h]
        gz2 = sm_ref[GZ2, :, c]
        gz2b = gz2.astype(BF)
        g2b = (gz2 * d["rp"]).astype(BF)
        dm = dmixed[:, c]
        gate = so_ref[GATE, :, c]
        n_o, inv_o = so_ref[NO, :, c], so_ref[INVO, :, c]
        n_a, inv_a = so_ref[NA, :, c], so_ref[INVA, :, c]
        gated, gate_slope = gelu_two(gate)
        d["dgate"] = dm * n_o * gp * gate_slope
        drm = dm * gated
        d["dgp"] = jnp.sum(drm * n_o, axis=0, keepdims=True)
        dpg = drm * gp
        do = (dpg - n_o * hv.mean(dpg * n_o)) * inv_o
        dn = do * g
        both = hv.mean(cat([dn, dn * n_a], 0))
        da2 = (dn - both[:length] - n_a * both[length:]) * inv_a
        d["dg"] = jnp.sum(do * n_a, axis=0, keepdims=True)
        d["dbe"] = jnp.sum(do, axis=0, keepdims=True)
        d["db2"] = jnp.sum(da2, axis=0, keepdims=True)
        da2b = da2.astype(BF)
        da2m, g2m = hv.split(da2b), hv.split(g2b)
        km = hv.split(kb)

        def weigh(mask, full, i):
            return (mask * full[length * i : length * (i + 1)]).astype(BF)

        p2 = dot_t(da2m, g2b)
        p2t = dot_t(g2m, da2b)
        dy2 = dot(da2b, d["w2"]) - cat(by_head(lambda e, i: dot(weigh(near, p2, i), x2[:, e])), 1)
        d["bx2"] = cat(by_head(lambda e, i: dot(weigh(near_t, p2t, i), y2[:, e])), 1)
        syt = by_head(lambda e, i: (near_t * (dot_t(x2[:, e], y2[:, e]) + 1.0)).astype(BF))
        d["bg2"] = -hv.both(syt, da2b)
        da1 = dy2 * e1_ref[:, h].astype(F32)
        da1b = da1.astype(BF)
        d["db1"] = jnp.sum(da1, axis=0, keepdims=True)
        p1 = by_head(lambda e, i: (near * dot_t(da1b[:, e], g1[:, e])).astype(BF))
        p1t = by_head(lambda e, i: (near_t * dot_t(g1[:, e], da1b[:, e])).astype(BF))
        d["dq"] = do + dot_t(da1b, d["w1"]) - hv.both(p1, kb)
        d["dk"] = -hv.both(p1t, qb)
        kq = dot_t(km, qb) + 1.0
        kk = dot_t(km, turned(kb)) + 1.0
        d["bg1"] = cat(by_head(lambda e, i: dot(weigh(near_t, kq, i), da1b[:, e])), 1)
        x2r, gz2r = turned(x2), turned(gz2b)
        d["m1t"] = [weigh(past_b, kk, i) for i in range(2)]
        d["rx"] = by_head(lambda e, i: (past_b * (dot_t(x2[:, e], x2r[:, e]) + 1.0)).astype(BF))
        ft = dot_t(g2m, gz2r)
        d["ft"] = [weigh(past_b, ft, i) for i in range(2)]
        d.update(x2=x2, y2=y2, g1=g1, g2b=g2b, gz2=gz2, gz2b=gz2b, x2r=x2r, gz2r=gz2r)
        d.update(kb=kb, qb=qb, da1b=da1b, da2b=da2b)
        for name in ("z1", "z2", "u", "rg1", "rg2", "t"):
            d[name] = [None] * steps
        st.append(d)
    for s in reversed(range(steps)):
        sl = slice(rows * s, rows * s + rows)
        later = length - rows * (s + 1)
        mask = past_b[sl, :later]
        for p in range(pairs):
            d = st[p]
            c, h = d["c"], d["h"]
            x2, x2e, g2e = d["x2"], d["x2"][: rows * s], d["g2b"][: rows * s]
            bg1, bg2, bx2 = -d["bg1"][sl], d["bg2"][sl], -d["bx2"][sl]
            if s < steps - 1:

                def full(parts):
                    return join(parts[: s : -1])

                z1l, z2l, ul = full(d["z1"]), full(d["z2"]), full(d["u"])
                x2l = d["x2r"][:later]
                bg1 = bg1 - cat(by_head(lambda e, i: dot(d["m1t"][i][sl, :later], z1l[:, e])), 1)
                xu = by_head(lambda e, i: (mask * dot_t(x2[sl, e], ul[:, e])).astype(BF))
                bg2 = bg2 - hv.both([d["rx"][i][sl, :later] for i in range(2)], z2l) - hv.both(xu, d["gz2r"][:later])
                gz = dot_t(hv.split(d["g2b"][sl]), z2l)
                bx2 = bx2 - cat(
                    by_head(
                        lambda e, i: dot((mask * gz[rows * i : rows * (i + 1)]).astype(BF), x2l[:, e])
                        + dot(d["ft"][i][sl, :later], ul[:, e])
                    ),
                    1,
                )
            r0, r1 = d["r"][0][sl], d["r"][1][sl]
            dgz1 = cat([bg1[:, :hid] * r0, bg1[:, hid:] * r1], 1)
            slope = d1_ref[sl, h].astype(F32)
            du = dgz1 * slope
            dub = du.astype(BF)
            dz1 = dgz1 * ud2_ref[sl, h].astype(F32)
            dgz2 = bg2 * d["rp"][sl] + dot_t(dub, d["w2"])
            if s:
                hm = by_head(lambda e, i: (past[sl, : rows * s] * dot_t(dub[:, e], x2e[:, e])).astype(BF))
                dgz2 = dgz2 - hv.both(hm, g2e)
            n, inv = sm_ref[NRM, sl, c], sm_ref[INV, sl, c]
            mis, mn = sm_ref[MIS, sl, c], sm_ref[MEANN, sl, c]
            g = d["g"]
            e = dgz2 * inv
            three = hv.mean(cat([e, e * n, dgz2 * d["gz2"][sl]], 0))
            dmis = e - three[:rows] - n * three[rows : 2 * rows]
            t = dmis * g
            dn = t * g - e * mn - mis * g * three[rows : 2 * rows]
            two = hv.mean(cat([dn, dn * n], 0))
            dz2 = inv * (dn - two[:rows] - n * (two[rows:] + three[2 * rows :]))
            d["dg"] = d["dg"] + jnp.sum(t * n + dmis * mis, axis=0, keepdims=True)
            d["dbe"] = d["dbe"] + jnp.sum(t, axis=0, keepdims=True)
            d["db2"] = d["db2"] + jnp.sum(dz2, axis=0, keepdims=True)
            dz2b = dz2.astype(BF)
            dx2 = bx2 + dot(dz2b, d["w2"])
            if s:
                j = dot_t(hv.split(dz2b), g2e)
                dx2 = dx2 - cat(
                    by_head(
                        lambda e, i: dot((past[sl, : rows * s] * j[rows * i : rows * (i + 1)]).astype(BF), x2e[:, e])
                    ),
                    1,
                )
            dz1 = dz1 + dx2 * slope
            d["db1"] = d["db1"] + jnp.sum(dz1, axis=0, keepdims=True)
            d["z1"][s], d["z2"][s], d["u"][s] = dz1.astype(BF), dz2b, dub
            d["rg1"][s], d["rg2"][s], d["t"][s] = bg1, bg2, t
    parts = [[], [], [], []]
    rate_cols = []
    for p in range(pairs):
        d = st[p]
        z1, z2, u = cat(d["z1"], 0), cat(d["z2"], 0), cat(d["u"], 0)
        t = cat(d["t"], 0)
        g1 = d["g1"]
        both = by_head(
            lambda e, i: (past * dot_t(z1[:, e], g1[:, e]) + past_t * dot_t(g1[:, e], z1[:, e])).astype(BF)
        )
        dk = d["dk"] + t + dot_t(z1, d["w1"]) - hv.both(both, d["kb"])
        for i, value in enumerate((d["dq"], dk, -t, d["dgate"])):
            parts[i].append(value.astype(BF))
        dw1 = tdot(cat([d["kb"], d["qb"]], 0), cat([z1, d["da1b"]], 0))
        dw2 = tdot(cat([z2, d["da2b"], d["gz2b"]], 0), cat([d["x2"], d["y2"], u], 0))
        for i in range(2):
            row = 64 * (2 * p + i)
            ig_ref[row : row + 64, :] = dw1[64 * i : 64 * i + 64, hid * i : hid * (i + 1)].astype(BF)
            row = row + 64 * heads
            ig_ref[row : row + 64, :] = dw2[64 * i : 64 * i + 64, hid * i : hid * (i + 1)].astype(BF)
            row = HIDDEN_ROW + 2 * p + i
            ms_ref[row : row + 1, :] = d["db1"][:, hid * i : hid * (i + 1)]
        one = cat(d["rg1"], 0) * g1.astype(F32)
        two = cat(d["rg2"], 0) * d["g2b"].astype(F32)
        two = cat([jnp.where(hv.left, two, 0.0), jnp.where(hv.left, 0.0, two)], 1)
        for i in range(2):
            whole = one[:, hid * i : hid * i + 128] + one[:, hid * i + 128 : hid * (i + 1)]
            whole = whole + two[:, 128 * i : 128 * (i + 1)]
            rate_cols.append(jnp.sum(whole, axis=-1, keepdims=True))
        for j, name in enumerate(("db2", "dg", "dgp", "dbe")):
            piece = 3 * j + p
            row = HEAD_ROW + piece // 2
            ms_ref[row : row + 1, 128 * (piece % 2) : 128 * (piece % 2) + 128] = d[name]
    lane = lax.broadcasted_iota(jnp.int32, (1, 16), 1)
    dlog = jnp.zeros((length, 16), F32)
    for i, col in enumerate(rate_cols):
        dlog = dlog + jnp.where(lane == i, col, 0.0)
    dlog = dlog * (1.0 - sg)
    ms_ref[OFFSET_ROW : OFFSET_ROW + 1, 0:16] = jnp.sum(dlog, axis=0, keepdims=True)
    dmix = [cat(x, 1) for x in parts]
    return dmix, dlog.astype(BF)


def ka_body(layer, *args):
    if layer == 0:
        dl_ref, li_ref = args[:2]
        rest = args[2:]
    else:
        dl_ref, h1_ref, fo_ref, fr_ref = args[:4]
        rest = args[4:]
    wrefs, rest = rest[:10], rest[10:]
    if layer == 1:
        lo_ref, rest = rest[0], rest[1:]
    hb_ref, x1_ref, att_ref = rest[:3]
    saves, scratch = rest[3:15], rest[15:]
    mix_v, inner_v, small_v, rate_v, out_v, sems = scratch[:6]
    pick = Pick(layer, sems)
    c_small = pick.start(wrefs[0], wrefs[1], small_v)
    c_mix = pick.start(wrefs[2], wrefs[3], mix_v)
    c_rate = pick.start(wrefs[4], wrefs[5], rate_v)
    c_inner = pick.start(wrefs[6], wrefs[7], inner_v)
    c_out = pick.start(wrefs[8], wrefs[9], out_v)
    length = hb_ref.shape[0]
    steps = length // (2 * MBT)
    begin, cut = doc_places(dl_ref, steps)
    places = block_starts(begin, steps)
    if layer == 0:
        low = gather_rows(li_ref, lax.axis_index("segment"), places)
    else:
        low = (h1_ref[...] + (fo_ref[...].astype(F32) + fr_ref[...].astype(F32))).astype(BF)
        scatter_rows(lo_ref, places, low)
        lo_ref.send()
    hb_ref[...] = low
    hb_ref.send()
    h = low.astype(F32)
    inv = rms_inv(h)
    c_small.wait()
    x_one = (h * inv * small_v[1:2, 0 : h.shape[1]]).astype(BF)
    x1_ref[...] = x_one
    x1_ref.send()
    c_mix.wait()
    c_rate.wait()
    c_inner.wait()
    forward = mixer_unrolled if layer else mixer_forward
    mixed = forward(saves, x_one, mix_v, rate_v, inner_v, small_v, (begin, cut), scratch[6:])
    c_out.wait()
    att_ref[...] = dot(mixed, out_v[...]).astype(BF)


def ffn_forward(h1, small_v, sw_v, dn_v, copies):
    width = h1.shape[1]
    inv = rms_inv(h1)
    x2 = (h1 * inv * small_v[1:2, width : 2 * width]).astype(BF)
    copies[0].wait()
    up_at = sw_v.shape[1] // 2
    gate = dot(x2, sw_v[:, :up_at])
    up = dot(x2, sw_v[:, up_at:])
    sgm = 1.0 / (1.0 + jnp.exp(-gate))
    silu = gate * sgm
    slope = up * (sgm * (1.0 + gate * (1.0 - sgm)))
    hidden = (silu * up).astype(BF)
    copies[1].wait()
    feed = dot(hidden, dn_v[...]).astype(BF)
    return x2, hidden, slope, silu, feed


def ffn_backward(dfe, slope, silu, sw_v, dn_v):
    up_at = sw_v.shape[1] // 2
    dh = dot_t(dfe, dn_v[...])
    dg, du = (dh * slope).astype(BF), (dh * silu).astype(BF)
    dx = dot_t(dg, sw_v[:, :up_at]) + dot_t(du, sw_v[:, up_at:])
    return dg, du, dx.astype(BF)


def pack_ffn(keep_ref, send_ref, x2, dg, du, hidden, dfe):
    first = lax.axis_index("segment") == 0
    width, wide = x2.shape[1], dg.shape[1]
    half = wide // 2

    def put(ref, grad, hid):
        ref[:, 0:width] = x2
        ref[:, width : width + wide] = grad
        ref[:, width + wide : width + wide + half] = hid
        ref[:, width + wide + half :] = dfe

    @pl.when(first)
    def _():
        put(keep_ref, dg, hidden[:, :half])
        put(send_ref, du, hidden[:, half:])

    @pl.when(jnp.logical_not(first))
    def _():
        put(keep_ref, du, hidden[:, half:])
        put(send_ref, dg, hidden[:, :half])


def kf_body(hb_ref, ao_ref, ar_ref, s_own, s_oth, w_own, w_oth, d_own, d_oth,
            h1_ref, x2_ref, hid_ref, sl_ref, si_ref, fe_ref, small_v, sw_v, dn_v, sems):
    pick = Pick(0, sems)
    c_small = pick.start(s_own, s_oth, small_v)
    copies = [pick.start(w_own, w_oth, sw_v), pick.start(d_own, d_oth, dn_v)]
    h1 = hb_ref[...].astype(F32) + (ao_ref[...].astype(F32) + ar_ref[...].astype(F32))
    h1_ref[...] = h1
    h1_ref.send()
    c_small.wait()
    x2, hidden, slope, silu, feed = ffn_forward(h1, small_v, sw_v, dn_v, copies)
    x2_ref[...] = x2
    hid_ref[...] = hidden
    sl_ref[...] = slope.astype(BF)
    si_ref[...] = silu.astype(BF)
    fe_ref[...] = feed


def kfb_body(dl_ref, ct_ref, hb_ref, ao_ref, ar_ref, s_own, s_oth, w_own, w_oth, d_own, d_oth,
             h1_ref, fe_ref, dxt_ref, dfe_ref, keep_ref, send_ref, small_v, sw_v, dn_v, sems):
    pick = Pick(1, sems)
    c_small = pick.start(s_own, s_oth, small_v)
    copies = [pick.start(w_own, w_oth, sw_v), pick.start(d_own, d_oth, dn_v)]
    length = hb_ref.shape[0]
    steps = length // (2 * MBT)
    begin, _ = doc_places(dl_ref, steps)
    dfe = gather_rows(ct_ref, lax.axis_index("segment"), block_starts(begin, steps))
    dfe_ref[...] = dfe
    h1 = hb_ref[...].astype(F32) + (ao_ref[...].astype(F32) + ar_ref[...].astype(F32))
    h1_ref[...] = h1
    h1_ref.send()
    c_small.wait()
    x2, hidden, slope, silu, feed = ffn_forward(h1, small_v, sw_v, dn_v, copies)
    fe_ref[...] = feed
    dg, du, dx = ffn_backward(dfe, slope, silu, sw_v, dn_v)
    dxt_ref[...] = dx
    pack_ffn(keep_ref, send_ref, x2, dg, du, hidden, dfe)


def norm_back(dx, x, gain, base):
    inv = rms_inv(x)
    e = dx * gain
    grad = base + e * inv - x * (jnp.mean(e * x, axis=-1, keepdims=True) * inv * inv * inv)
    gain_grad = jnp.sum(dx * x * inv, axis=0, keepdims=True)
    return grad, gain_grad


def kbf_body(dl_ref, hb_ref, dh_ref, xo_ref, xr_ref, t_own, t_oth, x2_ref, hid_ref, sl_ref, si_ref,
             w_own, w_oth, d_own, d_oth,
             ig_ref, gg_ref, dfe_ref, dxt_ref, keep_ref, send_ref, small_v, sw_v, dn_v, sems, sems_two):
    above = Pick(1, sems)
    c_small = above.start(t_own, t_oth, small_v)
    pick = Pick(0, sems_two)
    copies = [pick.start(d_own, d_oth, dn_v), pick.start(w_own, w_oth, sw_v)]
    length, width = hb_ref.shape
    steps = length // (2 * MBT)
    begin, _ = doc_places(dl_ref, steps)
    dx = xo_ref[...].astype(F32) + xr_ref[...].astype(F32)
    c_small.wait()
    grad, gain = norm_back(dx, hb_ref[...].astype(F32), small_v[1:2, 0:width], dh_ref[...])
    scatter_rows(ig_ref, block_starts(begin, steps), grad)
    ig_ref.send()
    gg_ref[...] = gain
    dfe = grad.astype(BF)
    dfe_ref[...] = dfe
    for c in copies:
        c.wait()
    dg, du, dxt = ffn_backward(dfe, sl_ref[...].astype(F32), si_ref[...].astype(F32), sw_v, dn_v)
    dxt_ref[...] = dxt
    pack_ffn(keep_ref, send_ref, x2_ref[...], dg, du, hid_ref[...], dfe)


def stat_rows(own, other, dp):
    zero = lax.axis_index("tensor") == 0
    low, high = jnp.where(zero, own, other), jnp.where(zero, other, own)
    line = cat([low[0:1], high[0:1], low[1:2], high[1:2], jnp.zeros((1, 64), F32)], 1)
    core = lax.axis_index("segment")
    line = cat([jnp.where(core == 0, line, 0.0), jnp.where(core == 0, 0.0, line)], 1)
    row = lax.broadcasted_iota(jnp.int32, (dp, 256), 0)
    return jnp.where(row == lax.axis_index("dp"), line, 0.0)


def kba_body(layer, dp, dl_ref, xo_ref, xr_ref, dy_ref, h1_ref, x1_ref, mixed_ref, so_ref, sr_ref, *rest):
    saves, rest = rest[:10], rest[10:]
    wrefs, rest = rest[:10], rest[10:]
    dh_ref, dxo_ref, keep_ref, send_ref, ig_ref, ms_ref, mix_v, inner_v, small_v, rate_v, out_v, sems = rest
    pick = Pick(layer, sems)
    kq, x2, g1, y2, d1, ud2, e1, sm, so, sg = saves
    c_small = pick.start(wrefs[0], wrefs[1], small_v)
    h1_ref.start()
    c_out = pick.start(wrefs[8], wrefs[9], out_v)
    c_inner = pick.start(wrefs[6], wrefs[7], inner_v)
    for ref in (so, sg, sm, kq, x2, g1, y2, e1, d1, ud2, x1_ref, mixed_ref):
        ref.start()
    c_mix = pick.start(wrefs[2], wrefs[3], mix_v)
    c_rate = pick.start(wrefs[4], wrefs[5], rate_v)
    length, width = h1_ref.shape
    steps = length // (2 * MBT)
    place = doc_places(dl_ref, steps)
    dx = xo_ref[...].astype(F32) + xr_ref[...].astype(F32)
    c_small.wait()
    dh, gain = norm_back(dx, h1_ref[...], small_v[1:2, width : 2 * width], dy_ref[...].astype(F32))
    dh_ref[...] = dh
    dh_ref.send()
    ms_ref[...] = jnp.zeros(ms_ref.shape, F32)
    at = slice(2 * layer, 2 * layer + 2)
    ms_ref[STAT_ROW : STAT_ROW + dp, :] = stat_rows(so_ref[at, :], sr_ref[at, :], dp)
    for j in range(3):
        ms_ref[GAIN_ROW + j : GAIN_ROW + j + 1, :] = gain[:, 256 * j : 256 * j + 256]
    da = dh.astype(BF)
    c_out.wait()
    c_inner.wait()
    dmixed = dot_t(da, out_v[...])
    dmix, dlog = mixer_backward(dmixed, saves, inner_v, small_v, place, ig_ref, ms_ref)
    x1 = x1_ref[...]
    drate = tdot(dlog, x1)
    heads = inner_v.shape[0] // 2
    for j in range(3):
        row = RATE_ROW + heads * j
        ms_ref[row : row + heads, :] = drate[:heads, 256 * j : 256 * j + 256]
    c_mix.wait()
    c_rate.wait()
    dxo_ref[...] = (dot_t(cat(dmix, 1), mix_v[...]) + dot(dlog, rate_v[...])).astype(BF)
    first = lax.axis_index("segment") == 0
    half = width // 2
    wide = 2 * dmix[0].shape[1]
    mixed = mixed_ref[...]

    def put(ref, one, two, att):
        ref[:, 0:width] = x1
        ref[:, width : width + wide // 2] = one
        ref[:, width + wide // 2 : width + wide] = two
        ref[:, width + wide : width + wide + mixed.shape[1]] = mixed
        ref[:, width + wide + mixed.shape[1] :] = att

    @pl.when(first)
    def _():
        put(keep_ref, dmix[0], dmix[1], da[:, :half])
        put(send_ref, dmix[2], dmix[3], da[:, half:])

    @pl.when(jnp.logical_not(first))
    def _():
        put(keep_ref, dmix[2], dmix[3], da[:, half:])
        put(send_ref, dmix[0], dmix[1], da[:, :half])


def ke_body(dl_ref, hb_ref, dh_ref, xo_ref, xr_ref, s_own, s_oth, ig_ref, gg_ref, small_v, sems):
    pick = Pick(0, sems)
    c_small = pick.start(s_own, s_oth, small_v)
    length, width = hb_ref.shape
    steps = length // (2 * MBT)
    begin, _ = doc_places(dl_ref, steps)
    dx = xo_ref[...].astype(F32) + xr_ref[...].astype(F32)
    c_small.wait()
    grad, gain = norm_back(dx, hb_ref[...].astype(F32), small_v[1:2, 0:width], dh_ref[...])
    scatter_rows(ig_ref, block_starts(begin, steps), grad)
    gg_ref[...] = gain


def beside(one, two, low, high):
    return cat([one[:, low:high], two[:, low:high]], 0)


class Columns:
    def __init__(self, dst, buf, at, sems):
        self.dst, self.buf, self.at, self.sems, self.copies = dst, buf, at, sems, []

    def send(self, low, high):
        copy = pltpu.make_async_copy(
            self.buf.at[low:high], self.dst.at[low:high, self.at : self.at + self.buf.shape[1]],
            self.sems.at[len(self.copies)],
        )
        copy.start()
        self.copies.append(copy)

    def wait(self):
        for copy in self.copies:
            copy.wait()


def grad_ffn_body(kf_ref, rf_ref, out_ref, buf, sems):
    width, wide = 768, 1024
    half = wide // 2
    out = Columns(out_ref, buf, 0, sems)
    for k in range(2):
        rows = slice(384 * k, 384 * (k + 1))
        x = beside(kf_ref, rf_ref, 384 * k, 384 * (k + 1))
        buf[rows, :] = tdot(x, beside(kf_ref, rf_ref, width, width + wide)).astype(BF)
        out.send(384 * k, 384 * (k + 1))
    down = tdot(beside(kf_ref, rf_ref, width + wide, width + wide + half),
                beside(kf_ref, rf_ref, width + wide + half, 2 * width + wide + half)).astype(BF)
    buf[768:1152, 0:width] = down[0:384]
    for k in range(3):
        buf[768 + 128 * k : 768 + 128 * (k + 1), width:wide] = down[384:512, 256 * k : 256 * (k + 1)]
    out.send(768, PACK_ROWS)
    out.wait()


def grad_mix_body(pack_ref, ka_ref, ra_ref, ik_ref, ir_ref, out_ref, buf, sems):
    width = 768
    out = Columns(out_ref, buf, 1024, sems)
    base = lax.axis_index("segment") * 384
    for k in range(2):
        rows = slice(384 * k, 384 * (k + 1))
        x = beside(ka_ref, ra_ref, 384 * k, 384 * (k + 1))
        buf[rows, :] = tdot(x, beside(ka_ref, ra_ref, width, 2 * width)).astype(BF)
        out.send(384 * k, 384 * (k + 1))
    grad = tdot(beside(ka_ref, ra_ref, 1536, 1920), beside(ka_ref, ra_ref, 1920, 2304)).astype(BF)
    buf[768:960, 0:384] = grad[0:192]
    buf[768:960, 384:768] = grad[192:384]
    for k in range(3):
        rows = pl.ds(pl.multiple_of(base + 128 * k, 128), 128)
        value = ik_ref[rows, :].astype(F32) + ir_ref[rows, :].astype(F32)
        buf[960:1088, 256 * k : 256 * (k + 1)] = value.astype(BF)
    buf[1088:PACK_ROWS, :] = jnp.zeros((PACK_ROWS - 1088, width), BF)
    out.send(768, PACK_ROWS)
    out.wait()


def final_body(turn, in_ref, sw_ref, dn_ref, mx_ref, ow_ref, ex_ref, co_ref, buf, sems):
    copies = []
    rows = PACK_ROWS // 8
    for k in range(8):
        at = rows * k
        if turn:
            at = pl.multiple_of(lax.rem(k + lax.axis_index("segment"), 8) * rows, 16)
        copies.append(pltpu.make_async_copy(in_ref.at[pl.ds(at, rows)], buf.at[rows * k : rows * (k + 1)], sems.at[k]))
    for copy in copies:
        copy.start()
    ready = 0

    def wait(upto):
        nonlocal ready
        while ready * rows < upto:
            copies[ready].wait()
            ready += 1

    for h in range(4):
        wait(192 * (h + 1))
        part = slice(192 * h, 192 * (h + 1))
        for c in range(2):
            base = 1792 * c
            sw_ref[part, c, :] = buf[part, base : base + 1024].astype(F32)
            for j in range(2):
                at = base + 1024 + 384 * j
                mx_ref[part, 2 * c + j, :] = buf[part, at : at + 384].astype(F32)
        sw_ref.send(192 * h, 192 * (h + 1))
        mx_ref.send(192 * h, 192 * (h + 1))
    wait(PACK_ROWS)
    for c in range(2):
        base = 1792 * c
        dn_ref[512 * c : 512 * c + 384, :] = buf[768:1152, base : base + 768].astype(F32)
        for k in range(3):
            part = buf[768 + 128 * k : 768 + 128 * (k + 1), base + 768 : base + 1024]
            dn_ref[512 * c + 384 : 512 * (c + 1), 256 * k : 256 * (k + 1)] = part.astype(F32)
        dn_ref.send(512 * c, 512 * (c + 1))
        base = base + 1024
        for j in range(2):
            at = base + 384 * j
            ow_ref[192 * j : 192 * (j + 1), 384 * c : 384 * (c + 1)] = buf[768:960, at : at + 384].astype(F32)
        ref = (ex_ref, co_ref)[c]
        for k in range(3):
            ref[128 * k : 128 * (k + 1), :] = buf[960:1088, base + 256 * k : base + 256 * (k + 1)].astype(F32)


class Loaded:
    def __init__(self, src, buf, sem):
        self.buf, self.shape = buf, buf.shape
        self.copy = pltpu.make_async_copy(src, buf, sem)
        self.started, self.waiting = False, True

    def start(self):
        if not self.started:
            self.copy.start()
            self.started = True

    def __getitem__(self, at):
        if self.waiting:
            self.start()
            self.copy.wait()
            self.waiting = False
        return self.buf[at]


class Stored:
    def __init__(self, dst, buf, sems):
        self.dst, self.buf, self.sems, self.shape = dst, buf, sems, buf.shape
        self.parts = []

    def __setitem__(self, at, value):
        self.buf[at] = value

    def send(self, low=None, high=None):
        k = len(self.parts)
        if low is None:
            copy = pltpu.make_async_copy(self.buf, self.dst, self.sems.at[k])
        else:
            at = slice(low, high)
            copy = pltpu.make_async_copy(self.buf.at[at], self.dst.at[at], self.sems.at[k])
        copy.start()
        self.parts.append(copy)

    def wait(self):
        for copy in self.parts:
            copy.wait()


def in_hbm(x):
    return pltpu.with_memory_space_constraint(x, pltpu.HBM)


def call(body, name, ins, specs, outs, scratch=(), deps=(), vmem=36, lazy=False):
    ins = [in_hbm(x) if spec is LOAD or spec is HBM else x for x, spec in zip(ins, specs)]
    deps = [in_hbm(x) for x in deps]
    have, extra, results, own = len(ins), len(deps), len(outs), len(scratch)
    loads = [k for k, spec in enumerate(specs) if spec is LOAD]
    stores = [k for k, out in enumerate(outs) if len(out) == 3]
    buffers = [pltpu.VMEM(ins[k].shape, ins[k].dtype) for k in loads]
    buffers += [pltpu.VMEM(outs[k][0], outs[k][1]) for k in stores]
    sems = [pltpu.SemaphoreType.DMA((max(1, len(loads)),))]
    sems += [pltpu.SemaphoreType.DMA((outs[k][2],)) for k in stores]

    def inside(*refs):
        operands, rest = list(refs[:have]), refs[have + extra :]
        written, rest = list(rest[:results]), rest[results:]
        own_refs, rest = rest[:own], rest[own:]
        bufs, (load_sems, *store_sems) = rest[: len(buffers)], rest[len(buffers) :]
        for i, k in enumerate(loads):
            operands[k] = Loaded(operands[k], bufs[i], load_sems.at[i])
            if not lazy:
                operands[k].start()
        done = []
        for i, k in enumerate(stores):
            written[k] = Stored(written[k], bufs[len(loads) + i], store_sems[i])
            done.append(written[k])
        body(*operands, *written, *own_refs)
        for one in done:
            if not one.parts:
                one.send()
        for one in done:
            one.wait()
        for k in loads:
            operands[k][0:1]

    return pl.pallas_call(
        inside,
        out_shape=[(pltpu.HBM if len(o) == 3 else jax.ShapeDtypeStruct)(o[0], o[1]) for o in outs],
        in_specs=[HBM if spec is LOAD else spec for spec in specs] + [HBM] * extra,
        out_specs=[HBM if len(o) == 3 else VMEM for o in outs],
        scratch_shapes=list(scratch) + buffers + sems,
        compiler_params=pltpu.CompilerParams(vmem_limit_bytes=vmem * 1024 * 1024),
        cost_estimate=pl.CostEstimate(flops=0, bytes_accessed=0, transcendentals=0),
        name=name,
    )(*ins, *deps)


def gate_body(*refs):
    pass


def pack_body(hb_ref, ng_ref, ro_ref, rb_ref, hg_ref, hs_ref, rw_ref, ex_ref, co_ref, small_ref, rate_ref, inner_ref):
    heads, hid, width = ex_ref.shape[0], ex_ref.shape[2], ng_ref.shape[1]
    wide = 64 * heads
    small_ref[...] = jnp.zeros(small_ref.shape, F32)
    for k in range(2):
        small_ref[1:2, width * k : width * (k + 1)] = ng_ref[k : k + 1, :]
    small_ref[3:4, 0:heads] = ro_ref[...]
    for h in range(heads):
        small_ref[0:1, hid * h : hid * (h + 1)] = hb_ref[h]
        at = slice(64 * h, 64 * (h + 1))
        small_ref[2:3, at] = rb_ref[h]
        for k in range(2):
            small_ref[2:3, wide * (k + 1) + 64 * h : wide * (k + 1) + 64 * (h + 1)] = hg_ref[h, k : k + 1, :]
        small_ref[2:3, wide * 3 + 64 * h : wide * 3 + 64 * (h + 1)] = hs_ref[h]
    rate_ref[...] = jnp.zeros(rate_ref.shape, BF)
    rate_ref[0:heads, :] = rw_ref[...]
    inner_ref[0:heads] = ex_ref[...].astype(BF)
    inner_ref[heads:] = co_ref[...].astype(BF)


def swap(value, axis):
    return lax.ppermute(value, axis, [(0, 1), (1, 0)])


def shards(
    layer_input, doc_lengths, norm_gains, mixing, rate_weight, rate_offset, expand, hidden_bias, contract,
    result_bias, head_gains, head_shift, output_proj, swiglu, down_proj, cotangent,
):
    micro, _, length, width = layer_input.shape
    heads = rate_weight.shape[2]
    hid = expand.shape[3]
    wide = heads * 64
    ff = down_proj.shape[1]
    first = lax.axis_index("segment") == 0
    dl = doc_lengths.reshape(micro, 3)
    li = layer_input.reshape(micro, length, width)
    ct = cotangent.reshape(micro, length, width)
    mix = mixing[0].reshape(width, -1)
    ow = output_proj[0]
    dn = down_proj[0]
    small, rate, inner = call(
        pack_body, "pack",
        [hidden_bias.reshape(heads, 1, hid), norm_gains[0], rate_offset, result_bias.reshape(heads, 1, 64),
         jnp.transpose(head_gains[0], (1, 0, 2)), head_shift.reshape(heads, 1, 64), rate_weight[0].T, expand[0],
         jnp.swapaxes(contract[0], 1, 2)],
        [VMEM] * 9, [((4, heads * hid), F32), ((16, width), BF), ((2 * heads, 64, hid), BF)])
    sw = swiglu[0].reshape(width, -1)

    def both(x):
        return in_hbm(x), in_hbm(swap(x, "segment"))

    small_p, mix_p, rate_p, inner_p, ow_p = both(small), both(mix), both(rate), both(inner), both(ow)
    sw = pl.pallas_call(
        gate_body, out_shape=pltpu.HBM(sw.shape, BF), in_specs=[HBM] * 6, out_specs=HBM,
        input_output_aliases={0: 0}, name="gate",
    )(sw, *[in_hbm(pair[1]) for pair in (small_p, mix_p, rate_p, inner_p, ow_p)])
    sw_p, dn_p = both(sw), both(dn)
    att_w = small_p + mix_p + rate_p + inner_p + ow_p
    tok = (length, width)
    save_shapes = [
        ((length, wide), BF, 1), ((2, 16), F32), ((length, 2 * wide), BF, 1),
        ((length, heads * hid), BF, 1), ((length, heads * hid), BF, 1), ((length, heads * hid), BF, 1),
        ((length, heads * hid), BF, 1), ((length, heads * hid), BF, 1), ((length, heads * hid), BF, 1),
        ((5, length, wide), F32, 1), ((5, length, wide), F32, 1), ((length, 16), F32, 1),
    ]
    sem = pltpu.SemaphoreType.DMA
    att_scratch = [
        pltpu.VMEM(mix.shape, BF), pltpu.VMEM(inner.shape, BF), pltpu.VMEM(small.shape, F32),
        pltpu.VMEM(rate.shape, BF), pltpu.VMEM(ow.shape, BF), sem((5,)),
    ]
    tall = (length, heads * hid)
    work = [pltpu.VMEM(tall, F32)] * 3 + [
        pltpu.VMEM((heads, length, length), BF), pltpu.VMEM((heads // 2, length, 128), BF),
        pltpu.VMEM((heads // 2, 128, 2 * hid), BF), pltpu.VMEM((length, length), F32), pltpu.VMEM((length, wide), F32),
        pltpu.VMEM((8, wide), F32),
    ]
    ffn_scratch = [pltpu.VMEM(small.shape, F32), pltpu.VMEM(sw.shape, BF), pltpu.VMEM(dn.shape, BF)]

    def ka(layer, ins):
        outs = [(tok, BF, 1), (tok, BF, 1), (tok, BF)] + save_shapes
        specs = [SMEM, LOAD] + [VMEM] * (len(ins) - 2) + [HBM] * 10
        if layer == 1:
            outs = [(tok, BF, 1)] + outs
        return call(functools.partial(ka_body, layer), f"mixer_fwd{layer}", list(ins) + list(att_w), specs, outs,
                    att_scratch + work)

    def exchange(x):
        return x, swap(x, "tensor")

    h0, x1_0, att, *save0 = ka(0, (dl, li))
    mixed0, stats0, save0 = save0[0], save0[1], save0[2:]
    ao, ar = exchange(att)
    h1_0, x2_0, hid_0, sl_0, si_0, fe = call(
        kf_body, "ffn_fwd0", [h0, ao, ar, *small_p, *sw_p, *dn_p], [LOAD] + [VMEM] * 2 + [HBM] * 6,
        [(tok, F32, 1), (tok, BF, 1)] + [((length, ff), BF, 1)] * 3 + [(tok, BF)], ffn_scratch + [sem((3,))])
    fo, fr = exchange(fe)
    lo0, hm, x1_1, att, *save1 = ka(1, (dl, h1_0, fo, fr))
    mixed1, stats1, save1 = save1[0], save1[1], save1[2:]
    ao, ar = exchange(att)
    pack_f = (length, 2 * width + ff + ff // 2)
    h1_1, fe, dxt, dfe1, keep, send = call(
        kfb_body, "ffn_both1", [dl, ct, hm, ao, ar, *small_p, *sw_p, *dn_p], [SMEM, LOAD, LOAD] + [VMEM] * 2 + [HBM] * 6,
        [(tok, F32, 1), (tok, BF), (tok, BF), (tok, BF), (pack_f, BF), (pack_f, BF)],
        ffn_scratch + [sem((3,))])

    dp = lax.axis_size("dp")
    ring = [0, 2, 4, 6, 7, 5, 3, 1] if dp == 8 else list(range(dp))

    stats = cat([stats0, stats1], 0)
    stats_in = swap(stats, "tensor")
    xo, xr = exchange(dxt)
    fo, fr = exchange(fe)
    pack_a = (length, width + 2 * wide + wide + width // 2)

    def kba(layer, xo, xr, dy, h1, x1, mixed, save, deps=()):
        return call(functools.partial(kba_body, layer, dp), f"mixer_bwd{layer}",
                    [dl, xo, xr, dy, h1, x1, mixed, stats, stats_in, *save, *att_w],
                    [SMEM] + [VMEM] * 3 + [LOAD] * 3 + [VMEM] * 2 + [LOAD] * 10 + [HBM] * 10,
                    [(tok, F32, 1), (tok, BF), (pack_a, BF), (pack_a, BF), ((2 * wide, hid), BF),
                     ((STAT_ROW + dp, hid), F32)],
                    att_scratch, deps, lazy=True)

    turn = 1 if dp == 8 else 0
    params = pltpu.CompilerParams(vmem_limit_bytes=36 * 1024 * 1024)
    pack_shape = (PACK_ROWS, ff + width)

    def grad_ffn(keep, send):
        return pl.pallas_call(
            grad_ffn_body, out_shape=pltpu.HBM(pack_shape, BF), in_specs=[VMEM] * 2, out_specs=HBM,
            scratch_shapes=[pltpu.VMEM((PACK_ROWS, ff), BF), sem((3,))], compiler_params=params, name="grad_ffn",
        )(keep, swap(send, "segment"))

    def grad_mix(pack, keep, send, ig):
        return pl.pallas_call(
            grad_mix_body, out_shape=pltpu.HBM(pack_shape, BF), in_specs=[HBM] + [VMEM] * 4, out_specs=HBM,
            scratch_shapes=[pltpu.VMEM((PACK_ROWS, width), BF), sem((3,))], compiler_params=params, name="grad_mix",
            input_output_aliases={0: 0},
        )(in_hbm(pack), keep, swap(send, "segment"), ig, swap(ig, "segment"))

    def scatter(pack, by):
        order = [ring[by:] + ring[:by]]
        return lax.psum_scatter(pack, "dp", scatter_dimension=0, axis_index_groups=order, tiled=True)

    pack1 = grad_ffn(keep, send)
    dh, dxo, keep, send, ig, misc1 = kba(1, xo, xr, dfe1, h1_1, x1_1, mixed1, save1, (pack1,))
    xo, xr = exchange(dxo)
    pack1 = grad_mix(pack1, keep, send, ig)
    part1 = scatter(pack1, turn)
    ig1, gg1, dfe0, dxt, keep, send = call(
        kbf_body, "ffn_bwd0",
        [dl, hm, dh, xo, xr, *small_p, x2_0, hid_0, sl_0, si_0, *sw_p, *dn_p],
        [SMEM, LOAD, LOAD] + [VMEM] * 2 + [HBM] * 2 + [LOAD] * 4 + [HBM] * 4,
        [(tok, F32, 1), ((1, width), F32), (tok, BF), (tok, BF), (pack_f, BF), (pack_f, BF)],
        ffn_scratch + [sem((1,)), sem((2,))], (pack1,))
    pack0 = grad_ffn(keep, send)
    xo, xr = exchange(dxt)
    after = (pack0,) if turn else (pack0, part1)
    dh, dxo, keep, send, ig, misc0 = kba(0, xo, xr, dfe0, h1_0, x1_0, mixed0, save0, after)
    xo, xr = exchange(dxo)
    pack0 = grad_mix(pack0, keep, send, ig)
    part0 = scatter(pack0, 0)
    ig0, gg0 = call(ke_body, "input_grad0", [dl, h0, dh, xo, xr, *small_p],
                    [SMEM, LOAD, LOAD] + [VMEM] * 2 + [HBM] * 2, [(tok, F32, 1), ((1, width), F32)],
                    [pltpu.VMEM(small.shape, F32), sem((1,))], (pack0,))

    left = jnp.where(first, part0, lax.ppermute(part1, "segment", [(0, 1)]))
    right = jnp.where(first, lax.ppermute(part0, "segment", [(1, 0)]), part1)
    whole = lax.all_gather(cat([left, right], 1), "dp", axis=0, axis_index_groups=[ring], tiled=True)

    def lo1_body(dl_ref, h1_ref, fo_ref, fr_ref, lo_ref):
        begin, _ = doc_places(dl_ref, length // (2 * MBT))
        low = (h1_ref[...] + (fo_ref[...].astype(F32) + fr_ref[...].astype(F32))).astype(BF)
        scatter_rows(lo_ref, block_starts(begin, length // (2 * MBT)), low)

    (lo1,) = call(lo1_body, "output1", [dl, h1_1, fo, fr], [SMEM, LOAD] + [VMEM] * 2, [(tok, BF, 1)], (), (pack0,))

    def two_rows(zero, one):
        mine, theirs = jnp.where(first, zero, one), swap(jnp.where(first, one, zero), "segment")
        return jnp.where(first, jnp.stack([mine, theirs]), jnp.stack([theirs, mine]))[None, :, None]

    layer_output = two_rows(lo0, lo1)
    input_grads = two_rows(ig0, ig1)
    total = cat([misc0, misc1, gg0.reshape(3, hid), gg1.reshape(3, hid)], 0)
    total = total + swap(total, "segment")
    for k in range(dp.bit_length() - 1):
        total = total + lax.ppermute(total, "dp", [(i, i ^ (1 << k)) for i in range(dp)])
    rows = STAT_ROW + dp
    tail = total[2 * rows :]
    misc = jnp.where(first, total[:rows], total[rows : 2 * rows])
    gain_one = jnp.where(first, tail[:3], tail[3:]).reshape(width)
    g_rate = cat([misc[RATE_ROW + heads * j : RATE_ROW + heads * (j + 1)] for j in range(3)], 1).T[None]
    g_hidden = misc[HIDDEN_ROW : HIDDEN_ROW + heads][None]
    tail = misc[HEAD_ROW : HEAD_ROW + 6].reshape(4, heads, 64)
    g_result, g_heads, g_shift = tail[0][None], tail[1:3][None], tail[3][None]
    g_offset = misc[OFFSET_ROW, :heads][None]
    g_gains = jnp.stack([gain_one, misc[GAIN_ROW : GAIN_ROW + 3].reshape(width)])[None]
    rate_stats = misc[STAT_ROW:].reshape(dp, micro, 128)[:, :, :64].reshape(dp, micro, 2, 2, 16)
    rate_stats = jnp.transpose(rate_stats[..., :heads], (1, 0, 2, 3, 4)).reshape(1, micro, dp, 2, 2 * heads)
    g_sw, g_dn, g_mix, g_out, g_expand, g_contract = call(
        functools.partial(final_body, turn), "final", [whole], [HBM],
        [((width, 2, ff), F32, 4), ((ff, width), F32, 2), ((width, 4, wide), F32, 4), ((wide, width), F32, 1),
         ((wide, hid), F32, 1), ((wide, hid), F32, 1)],
        [pltpu.VMEM(whole.shape, BF), sem((8,))], vmem=40)
    g_expand = g_expand.reshape(expand.shape)
    g_contract = jnp.swapaxes(g_contract.reshape(1, heads, 64, hid), 2, 3)
    return (
        layer_output, input_grads, g_gains, g_mix[None], g_rate, g_offset, g_expand, g_hidden, g_contract, g_result,
        g_heads, g_shift, g_out[None], g_sw[None], g_dn[None], rate_stats,
    )


def solution(mesh):
    placed = (
        P(None, "dp", None, None),
        P(None, "dp", None),
        P("segment", None, None),
        P("segment", None, None, "tensor"),
        P("segment", None, "tensor"),
        P("segment", "tensor"),
        P("segment", "tensor", None, None),
        P("segment", "tensor", None),
        P("segment", "tensor", None, None),
        P("segment", "tensor", None),
        P("segment", None, "tensor", None),
        P("segment", "tensor", None),
        P("segment", "tensor", None),
        P("segment", None, None, "tensor"),
        P("segment", "tensor", None),
        P(None, "dp", None, None),
    )
    return jax.shard_map(
        shards,
        mesh=mesh,
        in_specs=placed,
        out_specs=(
            P("segment", None, "dp", None, None),
            P("segment", None, "dp", None, None),
            P("segment", None, None),
            P("segment", None, None, "tensor"),
            P("segment", None, "tensor"),
            P("segment", "tensor"),
            P("segment", "tensor", None, None),
            P("segment", "tensor", None),
            P("segment", "tensor", None, None),
            P("segment", "tensor", None),
            P("segment", None, "tensor", None),
            P("segment", "tensor", None),
            P("segment", "tensor", None),
            P("segment", None, None, "tensor"),
            P("segment", "tensor", None),
            P("segment", None, None, None, None),
        ),
        check_vma=False,
    )
```

profile of v0, /device:TPU:0, one launch (start us, length us, event | category | flops | bytes accessed | tf_op | source)
XLA Modules:
  0.0 327.7 jit_solution(8951841137748899647)
XLA Ops:
  7.3 2.2 copy.53
  11.4 2.7 copy.54
  14.1 1.6 collective-permute-done.refs_3_.refs_1_.refs_4_.refs_5_.refs_6_.refs_20_
  15.8 0.7 copy-done.19
  16.7 1.5 copy-done.14
  18.6 0.9 copy-done.17
  19.9 18.2 %mixer_fwd0.1 = (bf16[128,768]{1,0:T(8,128)(2,1)}, bf16[128,768]{1,0:T(8,128)(2,1)}, bf16[128,768]{1,0:T(8,128)(2,1)S(1)}, bf16[128,384]{1,0:T(8,128)(2,1)}, f32...) custom-call(s32[2,3]{1,0:T(2,128)S(1)} %bitcast.67, ...), custom_call_target="tpu_custom_call" | custom-call | tf_op jit(solution)/shard_map/mixer_fwd0/pallas_call | solution.py:1108
  38.1 2.7 collective-permute-start.5
  40.8 5.4 %collective-permute-done.5.refs_2_ = bf16[128,768]{1,0:T(8,128)(2,1)S(1)} collective-permute-done((bf16[128,768]{1,0:T(8,128)(2,1)S(1)}, bf16[128,768]{1,0:T(8,128)(2,1)S(1)}, u32[]{:S(2)}, u32[]{:S(2)}) %collective-permute-start.5) | collective-permute-done | bytes 196640 | tf_op jit(solution)/shard_map/ppermute | solution.py:1145
  46.3 1.7 copy-done.15
  47.9 4.2 %ffn_fwd0.1 = (f32[128,768]{1,0:T(8,128)}, bf16[128,768]{1,0:T(8,128)(2,1)}, bf16[128,1024]{1,0:T(8,128)(2,1)}, bf16[128,1024]{1,0:T(8,128)(2,1)}, bf16[128,1024...) custom-call(bf16[128,768]{1,0:T(8,128)(2,1)} %get-tuple-element.91.refs_0_.refs_1_, ...), custom_call_target="tpu_custom_call" | custom-call | tf_op jit(solution)/shard_map/ffn_fwd0/pallas_call | solution.py:1108
  52.1 1.8 collective-permute-start.8
  53.9 4.9 %collective-permute-done.8.refs_3_ = bf16[128,768]{1,0:T(8,128)(2,1)S(1)} collective-permute-done((bf16[128,768]{1,0:T(8,128)(2,1)S(1)}, bf16[128,768]{1,0:T(8,128)(2,1)S(1)}, u32[]{:S(2)}, u32[]{:S(2)}) %collective-permute-start.8) | collective-permute-done | bytes 196640 | tf_op jit(solution)/shard_map/ppermute | solution.py:1145
  58.8 15.4 %mixer_fwd1.1 = (bf16[128,768]{1,0:T(8,128)(2,1)}, bf16[128,768]{1,0:T(8,128)(2,1)}, bf16[128,768]{1,0:T(8,128)(2,1)}, bf16[128,768]{1,0:T(8,128)(2,1)S(1)}, bf1...) custom-call(s32[2,3]{1,0:T(2,128)S(1)} %bitcast.68, ...), custom_call_target="tpu_custom_call" | custom-call | tf_op jit(solution)/shard_map/mixer_fwd1/pallas_call | solution.py:1108
  74.2 1.6 collective-permute-start.9
  75.8 4.2 %collective-permute-done.9.refs_4_ = bf16[128,768]{1,0:T(8,128)(2,1)S(1)} collective-permute-done((bf16[128,768]{1,0:T(8,128)(2,1)S(1)}, bf16[128,768]{1,0:T(8,128)(2,1)S(1)}, u32[]{:S(2)}, u32[]{:S(2)}) %collective-permute-start.9) | collective-permute-done | bytes 196640 | tf_op jit(solution)/shard_map/ppermute | solution.py:1145
  80.0 5.9 %ffn_both1.1 = (f32[128,768]{1,0:T(8,128)}, bf16[128,768]{1,0:T(8,128)(2,1)S(1)}, bf16[128,768]{1,0:T(8,128)(2,1)S(1)}, bf16[128,768]{1,0:T(8,128)(2,1)S(1)}, bf...) custom-call(s32[2,3]{1,0:T(2,128)S(1)} %bitcast.69, bf16[2,128,768]{2,1,0:T(8,128)(2,1)} %bitcast.98, ...), custom_call_target="tpu_custom_call" | custom-call | tf_op jit(solution)/shard_map/ffn_both1/pallas_call | solution.py:1108
  86.0 1.5 collective-permute-start.11
  88.2 1.9 grad_ffn.2.refs_29_.pack_ref
  90.1 3.2 collective-permute-done.12.refs_8_
  93.3 18.8 %mixer_bwd1.1 = (f32[128,768]{1,0:T(8,128)}, bf16[128,768]{1,0:T(8,128)(2,1)S(1)}, bf16[128,2304]{1,0:T(8,128)(2,1)S(1)}, bf16[128,2304]{1,0:T(8,128)(2,1)S(1)},...) custom-call(s32[2,3]{1,0:T(2,128)S(1)} %bitcast.70, bf16[128,768]{1,0:T(8,128)(2,1)S(1)} %get-tuple-element.100.refs_1_, ...), custom_call_target="tpu_custom_call" | custom-call | tf_op jit(solution)/shard_map/mixer_bwd1/pallas_call | solution.py:1108
  112.7 2.1 collective-permute-done.16.ir_ref
  114.8 1.6 grad_mix.2.refs_15_
  116.5 1.5 collective-permute-start.14
  118.0 5.5 %collective-permute-done.14.refs_4_ = bf16[128,768]{1,0:T(8,128)(2,1)S(1)} collective-permute-done((bf16[128,768]{1,0:T(8,128)(2,1)S(1)}, bf16[128,768]{1,0:T(8,128)(2,1)S(1)}, u32[]{:S(2)}, u32[]{:S(2)}) %collective-permute-start.14) | collective-permute-done | bytes 196640 | tf_op jit(solution)/shard_map/ppermute | solution.py:1145
  123.5 6.1 %ffn_bwd0.1 = (f32[128,768]{1,0:T(8,128)}, f32[1,768]{1,0:T(1,128)S(1)}, bf16[128,768]{1,0:T(8,128)(2,1)S(1)}, bf16[128,768]{1,0:T(8,128)(2,1)S(1)}, bf16[128,30...) custom-call(s32[2,3]{1,0:T(2,128)S(1)} %bitcast.71, bf16[128,768]{1,0:T(8,128)(2,1)} %get-tuple-element.96.refs_2_.refs_1_, ...), custom_call_target="tpu_custom_call" | custom-call | tf_op jit(solution)/shard_map/ffn_bwd0/pallas_call | solution.py:1108
  129.6 1.5 collective-permute-start.18
  131.2 0.7 collective-permute-done.17.rf_ref
  131.9 1.9 grad_ffn.3.refs_29_.pack_ref
  133.8 3.1 collective-permute-done.18.refs_2_
  136.9 18.5 %mixer_bwd0.1 = (f32[128,768]{1,0:T(8,128)}, bf16[128,768]{1,0:T(8,128)(2,1)S(1)}, bf16[128,2304]{1,0:T(8,128)(2,1)S(1)}, bf16[128,2304]{1,0:T(8,128)(2,1)S(1)},...) custom-call(s32[2,3]{1,0:T(2,128)S(1)} %bitcast.72, bf16[128,768]{1,0:T(8,128)(2,1)S(1)} %get-tuple-element.129.refs_1_, ...), custom_call_target="tpu_custom_call" | custom-call | tf_op jit(solution)/shard_map/mixer_bwd0/pallas_call | solution.py:1108
  156.0 2.1 collective-permute-done.20.ir_ref
  158.1 1.6 grad_mix.3.refs_4_.refs_7_
  159.8 5.9 %reduce-scatter.5.cloned.1.call-done = bf16[144,1792]{1,0:T(8,128)(2,1)} async-done(((bf16[1152,1792]{1,0:T(8,128)(2,1)}), bf16[144,1792]{1,0:T(8,128)(2,1)}) %reduce-scatter.5.cloned.1.call-update) | async-done | bytes 516112 | tf_op jit(solution)/shard_map/reduce_scatter | solution.py:1265
  165.7 1.8 collective-permute-start.28
  167.5 49.1 %reduce-scatter.3.cloned.1.call-done = bf16[144,1792]{1,0:T(8,128)(2,1)} async-done(((bf16[1152,1792]{1,0:T(8,128)(2,1)}), bf16[144,1792]{1,0:T(8,128)(2,1)}) %reduce-scatter.3.cloned.1.call-update) | async-done | bytes 516112 | tf_op jit(solution)/shard_map/reduce_scatter | solution.py:1265
  216.6 1.5 collective-permute-start.29
  218.0 1.1 broadcast_select_fusion.1
  219.1 1.4 collective-permute-done.29
  220.6 1.0 pad_maximum_fusion
  221.7 1.5 collective-permute-start.22
  223.2 0.6 collective-permute-start.10
  223.8 5.5 %collective-permute-done.22.refs_4_ = bf16[128,768]{1,0:T(8,128)(2,1)S(1)} collective-permute-done((bf16[128,768]{1,0:T(8,128)(2,1)S(1)}, bf16[128,768]{1,0:T(8,128)(2,1)S(1)}, u32[]{:S(2)}, u32[]{:S(2)}) %collective-permute-start.22) | collective-permute-done | bytes 196640 | tf_op jit(solution)/shard_map/ppermute | solution.py:1145
  229.3 2.6 input_grad0.1
  232.0 0.6 collective-permute-start.24
  232.6 1.1 select_bitcast_fusion
  233.8 2.3 output1.1
  236.1 1.0 select_bitcast_fusion.1
  237.6 1.4 collective-permute-start.25
  239.1 6.4 %collective-permute-done.25 = f32[102,256]{1,0:T(8,128)S(1)} collective-permute-done((f32[102,256]{1,0:T(8,128)S(1)}, f32[102,256]{1,0:T(8,128)S(1)}, u32[]{:S(2)}, u32[]{:S(2)}) %collective-permute-start.25) | collective-permute-done | bytes 104480 | tf_op jit(solution)/shard_map/ppermute | solution.py:1309
  245.6 0.8 maximum_select_fusion.1
  246.4 6.7 %collective-permute-done.26 = f32[102,256]{1,0:T(8,128)S(1)} collective-permute-done((f32[102,256]{1,0:T(8,128)S(1)}, f32[102,256]{1,0:T(8,128)S(1)}, u32[]{:S(2)}, u32[]{:S(2)}) %collective-permute-start.26) | collective-permute-done | bytes 104480 | tf_op jit(solution)/shard_map/ppermute | solution.py:1309
  253.1 1.9 collective-permute-start.27
  255.0 0.9 maximum_select_fusion
  256.0 7.3 %collective-permute-done.27 = f32[102,256]{1,0:T(8,128)S(1)} collective-permute-done((f32[102,256]{1,0:T(8,128)S(1)}, f32[102,256]{1,0:T(8,128)S(1)}, u32[]{:S(2)}, u32[]{:S(2)}) %collective-permute-start.27) | collective-permute-done | bytes 104480 | tf_op jit(solution)/shard_map/ppermute | solution.py:1309
  263.8 0.6 copy.47
  264.6 0.7 copy.52
  265.4 0.6 copy.50
  266.0 0.6 copy.49
  266.6 0.6 copy.51
  267.2 0.6 copy.48
  267.8 0.6 maximum_bitcast_fusion.1
  268.4 44.7 %all-gather.2.cloned.1.call-done.refs_0_ = bf16[1152,3584]{1,0:T(8,128)(2,1)} async-done(((bf16[144,3584]{1,0:T(8,128)(2,1)}), bf16[1152,3584]{1,0:T(8,128)(2,1)}) %all-gather.2.cloned.1.call-update) | async-done | bytes 8257552 | tf_op jit(solution)/shard_map/all_gather | solution.py:1291
  313.2 7.8 %final.1 = (f32[768,2,1024]{2,1,0:T(2,128)}, f32[1024,768]{1,0:T(8,128)}, f32[768,4,384]{2,1,0:T(4,128)}, f32[384,768]{1,0:T(8,128)}, f32[384,256]{1,0:T(8,128)}, /*index=5*/f32[384,256]{1,0:T(8,128)}) custom-call(bf16[1152,3584]{1,0:T(8,128)(2,1)} %all-gather.2.cloned.1.call-done.refs_0_), custom_call_target="tpu_custom_call" | custom-call | tf_op jit(solution)/shard_map/final/pallas_call | solution.py:1108
  (114 shorter events, 6.9 us)
Async XLA Ops:
  7.2 3.0 copy-start.2
  7.2 3.0 copy-start.3
  7.2 3.0 copy-start.7
  7.2 3.0 copy-start.8
  7.2 3.0 copy-start.10
  7.2 3.0 copy-start.9
  7.2 3.0 copy-start.11
  7.3 3.0 copy-start.6
  7.3 3.0 copy-start.12
  7.3 158.4 %reduce-scatter.5.cloned.1.call-start = ((), (), s32[]{:S(2)}) async-start(), calls=%async_computation.3 | async-start | bytes 4644864 | tf_op jit(solution)/shard_map/reduce_scatter | solution.py:1265
  7.3 2.8 copy-start.20
  7.3 4.0 %copy-start.21 = (bf16[1,768,2,1024]{3,2,1,0:T(2,128)(2,1)S(1)}, bf16[1,768,2,1024]{3,2,1,0:T(2,128)(2,1)}, u32[]{:S(2)}) copy-start(bf16[1,768,2,1024]{3,2,1,0:T(2,128)(2,1)} %param.29) | copy-start | bytes 9437188
  9.6 4.5 %copy-start.13 = (bf16[96,8,4,384]{3,1,2,0:T(8,128)(2,1)}, bf16[96,8,4,384]{3,1,2,0:T(8,128)(2,1)S(1)}, u32[]{:S(2)}) copy-start(bf16[96,8,4,384]{3,1,2,0:T(8,128)(2,1)S(1)} %copy.53) | copy-start | bytes 7077892
  9.6 6.2 %collective-permute-start.1 = (bf16[768,1536]{1,0:T(8,128)(2,1)S(1)}, bf16[768,1536]{1,0:T(8,128)(2,1)S(1)}, u32[]{:S(2)}, u32[]{:S(2)}) collective-permute-start(bf16[768,1536]{1,0:T(8,128)(2,1)S(1)} %bitcast.82), channel_id=1, source_target_pairs={{0,16},{16,0},{1,17},{17,1},{2,18},{18,2},{3,19},{19,3},{4,20},{20... | collective-permute-start | bytes 7077896 | tf_op jit(solution)/shard_map/ppermute | solution.py:1145
  10.1 5.6 %collective-permute-start.4 = (bf16[384,768]{1,0:T(8,128)(2,1)S(1)}, bf16[384,768]{1,0:T(8,128)(2,1)S(1)}, u32[]{:S(2)}, u32[]{:S(2)}) collective-permute-start(bf16[384,768]{1,0:T(8,128)(2,1)S(1)} %bitcast.95), channel_id=1, source_target_pairs={{0,16},{16,0},{1,17},{17,1},{2,18},{18,2},{3,19},{19,3},{4,20},{20... | collective-permute-start | bytes 1769480 | tf_op jit(solution)/shard_map/ppermute | solution.py:1145
  10.3 3.7 %copy-start = (bf16[12,64,256]{2,1,0:T(8,128)(2,1)}, bf16[12,64,256]{2,1,0:T(8,128)(2,1)S(1)}, u32[]{:S(2)}) copy-start(bf16[12,64,256]{2,1,0:T(8,128)(2,1)S(1)} %get-tuple-element.90.refs_8_.refs_10_.refs_25_) | copy-start | bytes 1179652
  10.3 3.7 %copy-start.1 = (f32[4,1536]{1,0:T(4,128)}, f32[4,1536]{1,0:T(4,128)S(1)}, u32[]{:S(2)}) copy-start(f32[4,1536]{1,0:T(4,128)S(1)} %get-tuple-element.88.refs_2_.refs_3_.refs_4_.refs_5_.refs_19_) | copy-start | bytes 73732
  10.4 3.7 %copy-start.4 = (bf16[16,768]{1,0:T(8,128)(2,1)}, bf16[16,768]{1,0:T(8,128)(2,1)S(1)}, u32[]{:S(2)}) copy-start(bf16[16,768]{1,0:T(8,128)(2,1)S(1)} %get-tuple-element.89.refs_6_.refs_8_.refs_23_) | copy-start | bytes 73732
  10.4 5.4 %collective-permute-start.3 = (bf16[12,64,256]{2,1,0:T(8,128)(2,1)S(1)}, bf16[12,64,256]{2,1,0:T(8,128)(2,1)S(1)}, u32[]{:S(2)}, u32[]{:S(2)}) collective-permute-start(bf16[12,64,256]{2,1,0:T(8,128)(2,1)S(1)} %get-tuple-element.90.refs_8_.refs_10_.refs_25_), channel_id=1, source_target_pairs={{0,16},{16,0},{1,17},{17,1},{2,18},{18,2},{3,19},{19,3},{4,20},{20... | collective-permute-start | bytes 1179656 | tf_op jit(solution)/shard_map/ppermute | solution.py:1145
  10.9 4.8 %collective-permute-start = (f32[4,1536]{1,0:T(4,128)S(1)}, f32[4,1536]{1,0:T(4,128)S(1)}, u32[]{:S(2)}, u32[]{:S(2)}) collective-permute-start(f32[4,1536]{1,0:T(4,128)S(1)} %get-tuple-element.88.refs_2_.refs_3_.refs_4_.refs_5_.refs_19_), channel_id=1, source_target_pairs={{0,16},{16,0},{1,17},{17,1},{2,18},{18,2},{3,19},{19,3},{4,20},{20... | collective-permute-start | bytes 73736 | tf_op jit(solution)/shard_map/ppermute | solution.py:1145
  10.9 4.8 %collective-permute-start.2 = (bf16[16,768]{1,0:T(8,128)(2,1)S(1)}, bf16[16,768]{1,0:T(8,128)(2,1)S(1)}, u32[]{:S(2)}, u32[]{:S(2)}) collective-permute-start(bf16[16,768]{1,0:T(8,128)(2,1)S(1)} %get-tuple-element.89.refs_6_.refs_8_.refs_23_), channel_id=1, source_target_pairs={{0,16},{16,0},{1,17},{17,1},{2,18},{18,2},{3,19},{19,3},{4,20},{20... | collective-permute-start | bytes 73736 | tf_op jit(solution)/shard_map/ppermute | solution.py:1145
  15.7 2.5 copy-start.22
  15.7 2.4 copy-start.23
  15.7 0.7 copy-start.19
  15.7 1.0 copy-start.16
  16.7 1.5 copy-start.14
  18.2 1.4 copy-start.17
  18.2 1.8 copy-start.5
  18.2 28.1 %collective-permute-start.6 = (bf16[768,2048]{1,0:T(8,128)(2,1)}, bf16[768,2048]{1,0:T(8,128)(2,1)S(1)}, u32[]{:S(2)}, u32[]{:S(2)}) collective-permute-start(bf16[768,2048]{1,0:T(8,128)(2,1)} %gate.1.refs_5_.refs_7_.refs_11_), channel_id=1, source_target_pairs={{0,16},{16,0},{1,17},{17,1},{2,18},{18,2},{3,19},{19,3},{4,20},{20... | collective-permute-start | bytes 9437192 | tf_op jit(solution)/shard_map/ppermute | solution.py:1145
  19.6 21.3 %collective-permute-start.7 = (bf16[1024,768]{1,0:T(8,128)(2,1)S(1)}, bf16[1024,768]{1,0:T(8,128)(2,1)S(1)}, u32[]{:S(2)}, u32[]{:S(2)}) collective-permute-start(bf16[1024,768]{1,0:T(8,128)(2,1)S(1)} %bitcast.90), channel_id=1, source_target_pairs={{0,16},{16,0},{1,17},{17,1},{2,18},{18,2},{3,19},{19,3},{4,20},{20... | collective-permute-start | bytes 4718600 | tf_op jit(solution)/shard_map/ppermute | solution.py:1145
  38.1 8.1 %collective-permute-start.5 = (bf16[128,768]{1,0:T(8,128)(2,1)S(1)}, bf16[128,768]{1,0:T(8,128)(2,1)S(1)}, u32[]{:S(2)}, u32[]{:S(2)}) collective-permute-start(bf16[128,768]{1,0:T(8,128)(2,1)S(1)} %get-tuple-element.92.refs_1_), channel_id=1, source_target_pairs={{0,1},{1,0},{2,3},{3,2},{4,5},{5,4},{6,7},{7,6},{8,9},{9,8},{10,11... | collective-permute-start | bytes 589832 | tf_op jit(solution)/shard_map/ppermute | solution.py:1145
  40.8 5.4 %copy-start.18 = (bf16[1024,768]{1,0:T(8,128)(2,1)}, bf16[1024,768]{1,0:T(8,128)(2,1)S(1)}, u32[]{:S(2)}) copy-start(bf16[1024,768]{1,0:T(8,128)(2,1)S(1)} %collective-permute-done.7.refs_8_.refs_10_.refs_14_) | copy-start | bytes 4718596
  46.3 1.7 copy-start.15
  52.1 6.7 %collective-permute-start.8 = (bf16[128,768]{1,0:T(8,128)(2,1)S(1)}, bf16[128,768]{1,0:T(8,128)(2,1)S(1)}, u32[]{:S(2)}, u32[]{:S(2)}) collective-permute-start(bf16[128,768]{1,0:T(8,128)(2,1)S(1)} %get-tuple-element.94.refs_2_), channel_id=1, source_target_pairs={{0,1},{1,0},{2,3},{3,2},{4,5},{5,4},{6,7},{7,6},{8,9},{9,8},{10,11... | collective-permute-start | bytes 589832 | tf_op jit(solution)/shard_map/ppermute | solution.py:1145
  74.2 5.8 %collective-permute-start.9 = (bf16[128,768]{1,0:T(8,128)(2,1)S(1)}, bf16[128,768]{1,0:T(8,128)(2,1)S(1)}, u32[]{:S(2)}, u32[]{:S(2)}) collective-permute-start(bf16[128,768]{1,0:T(8,128)(2,1)S(1)} %get-tuple-element.97.refs_3_), channel_id=1, source_target_pairs={{0,1},{1,0},{2,3},{3,2},{4,5},{5,4},{6,7},{7,6},{8,9},{9,8},{10,11... | collective-permute-start | bytes 589832 | tf_op jit(solution)/shard_map/ppermute | solution.py:1145
  85.9 2.4 collective-permute-start.13
  86.0 7.4 %collective-permute-start.11 = (bf16[128,768]{1,0:T(8,128)(2,1)S(1)}, bf16[128,768]{1,0:T(8,128)(2,1)S(1)}, u32[]{:S(2)}, u32[]{:S(2)}) collective-permute-start(bf16[128,768]{1,0:T(8,128)(2,1)S(1)} %get-tuple-element.100.refs_1_), channel_id=1, source_target_pairs={{0,1},{1,0},{2,3},{3,2},{4,5},{5,4},{6,7},{7,6},{8,9},{9,8},{10,11... | collective-permute-start | bytes 589832 | tf_op jit(solution)/shard_map/ppermute | solution.py:1145
  87.5 5.8 %collective-permute-start.12 = (f32[4,16]{1,0:T(4,128)S(1)}, f32[4,16]{1,0:T(4,128)S(1)}, u32[]{:S(2)}, u32[]{:S(2)}) collective-permute-start(f32[4,16]{1,0:T(4,128)S(1)} %pad_maximum_fusion.2.refs_7_), channel_id=1, source_target_pairs={{0,1},{1,0},{2,3},{3,2},{4,5},{5,4},{6,7},{7,6},{8,9},{9,8},{10,11... | collective-permute-start | bytes 776 | tf_op jit(solution)/shard_map/ppermute | solution.py:1145
  112.1 2.6 collective-permute-start.15
  112.2 2.6 collective-permute-start.16
  116.4 100.1 %reduce-scatter.3.cloned.1.call-start = ((), (), s32[]{:S(2)}) async-start(), calls=%async_computation.2 | async-start | bytes 4644864 | tf_op jit(solution)/shard_map/reduce_scatter | solution.py:1265
  116.5 7.0 %collective-permute-start.14 = (bf16[128,768]{1,0:T(8,128)(2,1)S(1)}, bf16[128,768]{1,0:T(8,128)(2,1)S(1)}, u32[]{:S(2)}, u32[]{:S(2)}) collective-permute-start(bf16[128,768]{1,0:T(8,128)(2,1)S(1)} %get-tuple-element.119.refs_3_), channel_id=1, source_target_pairs={{0,1},{1,0},{2,3},{3,2},{4,5},{5,4},{6,7},{7,6},{8,9},{9,8},{10,11... | collective-permute-start | bytes 589832 | tf_op jit(solution)/shard_map/ppermute | solution.py:1145
  129.5 2.4 collective-permute-start.17
  129.6 7.3 %collective-permute-start.18 = (bf16[128,768]{1,0:T(8,128)(2,1)S(1)}, bf16[128,768]{1,0:T(8,128)(2,1)S(1)}, u32[]{:S(2)}, u32[]{:S(2)}) collective-permute-start(bf16[128,768]{1,0:T(8,128)(2,1)S(1)} %get-tuple-element.129.refs_1_), channel_id=1, source_target_pairs={{0,1},{1,0},{2,3},{3,2},{4,5},{5,4},{6,7},{7,6},{8,9},{9,8},{10,11... | collective-permute-start | bytes 589832 | tf_op jit(solution)/shard_map/ppermute | solution.py:1145
  155.4 2.6 collective-permute-start.19
  155.6 2.4 collective-permute-start.20
  159.7 153.4 %all-gather.2.cloned.1.call-start = ((), (), s32[]{:S(2)}) async-start(), calls=%async_computation.4 | async-start | bytes 9289728 | tf_op jit(solution)/shard_map/all_gather | solution.py:1291
  165.7 52.4 %collective-permute-start.28 = (bf16[144,1792]{1,0:T(8,128)(2,1)}, bf16[144,1792]{1,0:T(8,128)(2,1)S(1)}, u32[]{:S(2)}, u32[]{:S(2)}) collective-permute-start(bf16[144,1792]{1,0:T(8,128)(2,1)} %reduce-scatter.5.cloned.1.call-done), channel_id=1, source_target_pairs={{0,16},{1,17},{2,18},{3,19},{4,20},{5,21},{6,22},{7,23},{8,24},{9,... | collective-permute-start | bytes 1548296 | tf_op jit(solution)/shard_map/ppermute | solution.py:1289
  216.6 4.0 %collective-permute-start.29 = (bf16[144,1792]{1,0:T(8,128)(2,1)}, bf16[144,1792]{1,0:T(8,128)(2,1)S(1)}, u32[]{:S(2)}, u32[]{:S(2)}) collective-permute-start(bf16[144,1792]{1,0:T(8,128)(2,1)} %reduce-scatter.3.cloned.1.call-done), channel_id=1, source_target_pairs={{16,0},{17,1},{18,2},{19,3},{20,4},{21,5},{22,6},{23,7},{24,8},{25... | collective-permute-start | bytes 1548296 | tf_op jit(solution)/shard_map/ppermute | solution.py:1290
  221.7 10.9 %copy-start.24 = (f32[128,768]{1,0:T(8,128)S(1)}, f32[128,768]{1,0:T(8,128)}, u32[]{:S(2)}) copy-start(f32[128,768]{1,0:T(8,128)} %get-tuple-element.149) | copy-start | bytes 1179652
  221.7 7.6 %collective-permute-start.22 = (bf16[128,768]{1,0:T(8,128)(2,1)S(1)}, bf16[128,768]{1,0:T(8,128)(2,1)S(1)}, u32[]{:S(2)}, u32[]{:S(2)}) collective-permute-start(bf16[128,768]{1,0:T(8,128)(2,1)S(1)} %get-tuple-element.147.refs_3_), channel_id=1, source_target_pairs={{0,1},{1,0},{2,3},{3,2},{4,5},{5,4},{6,7},{7,6},{8,9},{9,8},{10,11... | collective-permute-start | bytes 589832 | tf_op jit(solution)/shard_map/ppermute | solution.py:1145
  223.2 10.6 %collective-permute-start.10 = (bf16[128,768]{1,0:T(8,128)(2,1)S(1)}, bf16[128,768]{1,0:T(8,128)(2,1)S(1)}, u32[]{:S(2)}, u32[]{:S(2)}) collective-permute-start(bf16[128,768]{1,0:T(8,128)(2,1)S(1)} %get-tuple-element.99.refs_2_), channel_id=1, source_target_pairs={{0,1},{1,0},{2,3},{3,2},{4,5},{5,4},{6,7},{7,6},{8,9},{9,8},{10,11... | collective-permute-start | bytes 589832 | tf_op jit(solution)/shard_map/ppermute | solution.py:1145
  232.0 5.6 %collective-permute-start.24 = (f32[102,256]{1,0:T(8,128)S(1)}, f32[102,256]{1,0:T(8,128)S(1)}, u32[]{:S(2)}, u32[]{:S(2)}) collective-permute-start(f32[102,256]{1,0:T(8,128)S(1)} %pad_maximum_fusion.1), channel_id=1, source_target_pairs={{0,16},{16,0},{1,17},{17,1},{2,18},{18,2},{3,19},{19,3},{4,20},{20... | collective-permute-start | bytes 313352 | tf_op jit(solution)/shard_map/ppermute | solution.py:1145
  232.6 3.5 %copy-start.25 = (bf16[128,768]{1,0:T(8,128)(2,1)S(1)}, bf16[128,768]{1,0:T(8,128)(2,1)}, u32[]{:S(2)}) copy-start(bf16[128,768]{1,0:T(8,128)(2,1)} %get-tuple-element.95) | copy-start | bytes 589828
  233.7 21.4 %collective-permute-start.23 = (f32[128,768]{1,0:T(8,128)S(1)}, f32[128,768]{1,0:T(8,128)S(1)}, u32[]{:S(2)}, u32[]{:S(2)}) collective-permute-start(f32[128,768]{1,0:T(8,128)S(1)} %get-tuple-element.209), channel_id=1, source_target_pairs={{0,16},{16,0},{1,17},{17,1},{2,18},{18,2},{3,19},{19,3},{4,20},{20... | collective-permute-start | bytes 1179656 | tf_op jit(solution)/shard_map/ppermute | solution.py:1145
  237.1 8.5 %collective-permute-start.21 = (bf16[128,768]{1,0:T(8,128)(2,1)S(1)}, bf16[128,768]{1,0:T(8,128)(2,1)S(1)}, u32[]{:S(2)}, u32[]{:S(2)}) collective-permute-start(bf16[128,768]{1,0:T(8,128)(2,1)S(1)} %get-tuple-element.211), channel_id=1, source_target_pairs={{0,16},{16,0},{1,17},{17,1},{2,18},{18,2},{3,19},{19,3},{4,20},{20... | collective-permute-start | bytes 589832 | tf_op jit(solution)/shard_map/ppermute | solution.py:1145
  237.6 7.8 %collective-permute-start.25 = (f32[102,256]{1,0:T(8,128)S(1)}, f32[102,256]{1,0:T(8,128)S(1)}, u32[]{:S(2)}, u32[]{:S(2)}) collective-permute-start(f32[102,256]{1,0:T(8,128)S(1)} %fusion.1), channel_id=1, source_target_pairs={{0,2},{2,0},{4,6},{6,4},{8,10},{10,8},{12,14},{14,12},{1,3},{3,1},... | collective-permute-start | bytes 313352 | tf_op jit(solution)/shard_map/ppermute | solution.py:1309
  245.5 7.6 %collective-permute-start.26 = (f32[102,256]{1,0:T(8,128)S(1)}, f32[102,256]{1,0:T(8,128)S(1)}, u32[]{:S(2)}, u32[]{:S(2)}) collective-permute-start(f32[102,256]{1,0:T(8,128)S(1)} %add.17), channel_id=1, source_target_pairs={{0,4},{2,6},{4,0},{6,2},{8,12},{10,14},{12,8},{14,10},{1,5},{3,7},... | collective-permute-start | bytes 313352 | tf_op jit(solution)/shard_map/ppermute | solution.py:1309
  253.1 10.1 %collective-permute-start.27 = (f32[102,256]{1,0:T(8,128)S(1)}, f32[102,256]{1,0:T(8,128)S(1)}, u32[]{:S(2)}, u32[]{:S(2)}) collective-permute-start(f32[102,256]{1,0:T(8,128)S(1)} %add.18), channel_id=1, source_target_pairs={{0,8},{2,10},{4,12},{6,14},{8,0},{10,2},{12,4},{14,6},{1,9},{3,11}... | collective-permute-start | bytes 313352 | tf_op jit(solution)/shard_map/ppermute | solution.py:1309
Sparse Core Ops, SparseCore 0:
  116.5 49.0 reduce-scatter.4
  168.7 47.8 reduce-scatter.2
  221.8 91.3 all-gather.1
where the time goes:
time: 332 us; the launch traced here: 328 us
  waiting for transfers between devices  160 us (48%)
  Pallas kernels  107 us (32%)
  starting transfers between devices  25.1 us (8%)
  local copies, waits for them, and re-layouts  14.6 us (4%)
  between operations  14.5 us (4%)
  other arithmetic  6.73 us (2%)
    pallas_call x11, Pallas kernels, call(): pl.pallas_call(inside, out_shape=[(pltpu.HBM if len(o) == 3 else jax.Shap...  99.8 us
    reduce_scatter x2, waiting for transfers between devices, scatter(): lax.psum_scatter(pack, 'dp', scatter_dimension=0, axis_index_groups=order...  54.9 us
    all_gather x1, waiting for transfers between devices, shards(): lax.all_gather(cat([left, right], 1), 'dp', axis=0, axis_index_groups=[ri...  44.7 us
    ppermute x25, waiting for transfers between devices, swap(): return lax.ppermute(value, axis, [(0, 1), (1, 0)])  38.4 us
    ppermute x3, waiting for transfers between devices, shards(): lax.ppermute(total, 'dp', [(i, i ^ 1 << k) for i in range(dp)])  20.4 us
    ppermute x25, starting transfers between devices, swap(): return lax.ppermute(value, axis, [(0, 1), (1, 0)])  18.3 us
    unnamed x63, local copies, waits for them, and re-layouts  13.7 us
  transfers between devices with their start and end apart: 33, of which 19 were waited for; matrix products, arithmetic and copies ran while one was open for 4% of the time, Pallas kernels for 16%

commit v1 on v0

--- a/solution.py
+++ b/solution.py
@@ -381,7 +381,7 @@
     sg_ref.send()
 
     def step(s, carry, start=False):
-        at = slice(0, rows) if start else pl.ds(pl.multiple_of(s * rows, rows), rows)
+        at = slice(s * rows, (s + 1) * rows) if isinstance(s, int) else pl.ds(pl.multiple_of(s * rows, rows), rows)
         hv = Halves()
         mask = past_ref[at, :]
         rates = RATE * sg_ref.buf[at, :]
@@ -434,7 +434,8 @@
         return carry
 
     step(0, 0, True)
-    lax.fori_loop(1, steps, step, 0)
+    step(1, 0)
+    lax.fori_loop(2, steps, step, 0)
     for ref in (x2_ref, g1_ref, d1_ref, sm_ref):
         ref.send()
     mixed = []

time: 332 us -> 332 us (level)
  no operation moved by 1% of the time
where the time goes in v1:
time: 332 us; the launch traced here: 327 us
  waiting for transfers between devices  160 us (48%)
  Pallas kernels  106 us (32%)
  starting transfers between devices  25.1 us (8%)
  local copies, waits for them, and re-layouts  14.6 us (4%)
  between operations  14.5 us (4%)
  other arithmetic  6.73 us (2%)
    pallas_call x11, Pallas kernels, call(): pl.pallas_call(inside, out_shape=[(pltpu.HBM if len(o) == 3 else jax.Shap...  99.4 us
    reduce_scatter x2, waiting for transfers between devices, scatter(): lax.psum_scatter(pack, 'dp', scatter_dimension=0, axis_index_groups=order...  54.9 us
    all_gather x1, waiting for transfers between devices, shards(): lax.all_gather(cat([left, right], 1), 'dp', axis=0, axis_index_groups=[ri...  44.7 us
    ppermute x25, waiting for transfers between devices, swap(): return lax.ppermute(value, axis, [(0, 1), (1, 0)])  38.5 us
    ppermute x3, waiting for transfers between devices, shards(): lax.ppermute(total, 'dp', [(i, i ^ 1 << k) for i in range(dp)])  20.3 us
    ppermute x25, starting transfers between devices, swap(): return lax.ppermute(value, axis, [(0, 1), (1, 0)])  18.2 us
    unnamed x63, local copies, waits for them, and re-layouts  13.7 us
  transfers between devices with their start and end apart: 33, of which 19 were waited for; matrix products, arithmetic and copies ran while one was open for 4% of the time, Pallas kernels for 16%

profile of v1, /device:TPU:0, one launch (start us, length us, event | category | flops | bytes accessed | tf_op | source)
XLA Modules:
  0.0 327.2 jit_solution(6272159251970069920)
XLA Ops:
  7.3 2.2 copy.53
  11.4 2.7 copy.54
  14.1 1.6 collective-permute-done.refs_3_.refs_1_.refs_4_.refs_5_.refs_6_.refs_20_
  15.8 0.7 copy-done.19
  16.7 1.5 copy-done.14
  18.6 0.9 copy-done.17
  19.9 17.7 %mixer_fwd0.1 = (bf16[128,768]{1,0:T(8,128)(2,1)}, bf16[128,768]{1,0:T(8,128)(2,1)}, bf16[128,768]{1,0:T(8,128)(2,1)S(1)}, bf16[128,384]{1,0:T(8,128)(2,1)}, f32...) custom-call(s32[2,3]{1,0:T(2,128)S(1)} %bitcast.67, ...), custom_call_target="tpu_custom_call" | custom-call | tf_op jit(solution)/shard_map/mixer_fwd0/pallas_call | solution.py:1109
  37.7 2.7 collective-permute-start.5
  40.4 5.4 %collective-permute-done.5.refs_2_ = bf16[128,768]{1,0:T(8,128)(2,1)S(1)} collective-permute-done((bf16[128,768]{1,0:T(8,128)(2,1)S(1)}, bf16[128,768]{1,0:T(8,128)(2,1)S(1)}, u32[]{:S(2)}, u32[]{:S(2)}) %collective-permute-start.5) | collective-permute-done | bytes 196640 | tf_op jit(solution)/shard_map/ppermute | solution.py:1146
  45.8 1.7 copy-done.15
  47.5 4.2 %ffn_fwd0.1 = (f32[128,768]{1,0:T(8,128)}, bf16[128,768]{1,0:T(8,128)(2,1)}, bf16[128,1024]{1,0:T(8,128)(2,1)}, bf16[128,1024]{1,0:T(8,128)(2,1)}, bf16[128,1024...) custom-call(bf16[128,768]{1,0:T(8,128)(2,1)} %get-tuple-element.91.refs_0_.refs_1_, ...), custom_call_target="tpu_custom_call" | custom-call | tf_op jit(solution)/shard_map/ffn_fwd0/pallas_call | solution.py:1109
  51.7 1.8 collective-permute-start.8
  53.5 4.9 %collective-permute-done.8.refs_3_ = bf16[128,768]{1,0:T(8,128)(2,1)S(1)} collective-permute-done((bf16[128,768]{1,0:T(8,128)(2,1)S(1)}, bf16[128,768]{1,0:T(8,128)(2,1)S(1)}, u32[]{:S(2)}, u32[]{:S(2)}) %collective-permute-start.8) | collective-permute-done | bytes 196640 | tf_op jit(solution)/shard_map/ppermute | solution.py:1146
  58.4 15.4 %mixer_fwd1.1 = (bf16[128,768]{1,0:T(8,128)(2,1)}, bf16[128,768]{1,0:T(8,128)(2,1)}, bf16[128,768]{1,0:T(8,128)(2,1)}, bf16[128,768]{1,0:T(8,128)(2,1)S(1)}, bf1...) custom-call(s32[2,3]{1,0:T(2,128)S(1)} %bitcast.68, ...), custom_call_target="tpu_custom_call" | custom-call | tf_op jit(solution)/shard_map/mixer_fwd1/pallas_call | solution.py:1109
  73.8 1.6 collective-permute-start.9
  75.4 4.2 %collective-permute-done.9.refs_4_ = bf16[128,768]{1,0:T(8,128)(2,1)S(1)} collective-permute-done((bf16[128,768]{1,0:T(8,128)(2,1)S(1)}, bf16[128,768]{1,0:T(8,128)(2,1)S(1)}, u32[]{:S(2)}, u32[]{:S(2)}) %collective-permute-start.9) | collective-permute-done | bytes 196640 | tf_op jit(solution)/shard_map/ppermute | solution.py:1146
  79.6 5.9 %ffn_both1.1 = (f32[128,768]{1,0:T(8,128)}, bf16[128,768]{1,0:T(8,128)(2,1)S(1)}, bf16[128,768]{1,0:T(8,128)(2,1)S(1)}, bf16[128,768]{1,0:T(8,128)(2,1)S(1)}, bf...) custom-call(s32[2,3]{1,0:T(2,128)S(1)} %bitcast.69, bf16[2,128,768]{2,1,0:T(8,128)(2,1)} %bitcast.98, ...), custom_call_target="tpu_custom_call" | custom-call | tf_op jit(solution)/shard_map/ffn_both1/pallas_call | solution.py:1109
  85.5 1.5 collective-permute-start.11
  87.0 0.6 collective-permute-start.12
  87.8 1.9 grad_ffn.2.refs_29_.pack_ref
  89.7 3.2 collective-permute-done.12.refs_8_
  92.9 18.8 %mixer_bwd1.1 = (f32[128,768]{1,0:T(8,128)}, bf16[128,768]{1,0:T(8,128)(2,1)S(1)}, bf16[128,2304]{1,0:T(8,128)(2,1)S(1)}, bf16[128,2304]{1,0:T(8,128)(2,1)S(1)},...) custom-call(s32[2,3]{1,0:T(2,128)S(1)} %bitcast.70, bf16[128,768]{1,0:T(8,128)(2,1)S(1)} %get-tuple-element.100.refs_1_, ...), custom_call_target="tpu_custom_call" | custom-call | tf_op jit(solution)/shard_map/mixer_bwd1/pallas_call | solution.py:1109
  112.3 2.1 collective-permute-done.16.ir_ref
  114.3 1.6 grad_mix.2.refs_15_
  116.0 1.5 collective-permute-start.14
  117.5 5.5 %collective-permute-done.14.refs_4_ = bf16[128,768]{1,0:T(8,128)(2,1)S(1)} collective-permute-done((bf16[128,768]{1,0:T(8,128)(2,1)S(1)}, bf16[128,768]{1,0:T(8,128)(2,1)S(1)}, u32[]{:S(2)}, u32[]{:S(2)}) %collective-permute-start.14) | collective-permute-done | bytes 196640 | tf_op jit(solution)/shard_map/ppermute | solution.py:1146
  123.0 6.1 %ffn_bwd0.1 = (f32[128,768]{1,0:T(8,128)}, f32[1,768]{1,0:T(1,128)S(1)}, bf16[128,768]{1,0:T(8,128)(2,1)S(1)}, bf16[128,768]{1,0:T(8,128)(2,1)S(1)}, bf16[128,30...) custom-call(s32[2,3]{1,0:T(2,128)S(1)} %bitcast.71, bf16[128,768]{1,0:T(8,128)(2,1)} %get-tuple-element.96.refs_2_.refs_1_, ...), custom_call_target="tpu_custom_call" | custom-call | tf_op jit(solution)/shard_map/ffn_bwd0/pallas_call | solution.py:1109
  129.2 1.5 collective-permute-start.18
  130.7 0.8 collective-permute-done.17.rf_ref
  131.5 1.9 grad_ffn.3.refs_29_.pack_ref
  133.4 3.1 collective-permute-done.18.refs_2_
  136.5 18.5 %mixer_bwd0.1 = (f32[128,768]{1,0:T(8,128)}, bf16[128,768]{1,0:T(8,128)(2,1)S(1)}, bf16[128,2304]{1,0:T(8,128)(2,1)S(1)}, bf16[128,2304]{1,0:T(8,128)(2,1)S(1)},...) custom-call(s32[2,3]{1,0:T(2,128)S(1)} %bitcast.72, bf16[128,768]{1,0:T(8,128)(2,1)S(1)} %get-tuple-element.129.refs_1_, ...), custom_call_target="tpu_custom_call" | custom-call | tf_op jit(solution)/shard_map/mixer_bwd0/pallas_call | solution.py:1109
  155.6 2.1 collective-permute-done.20.ir_ref
  157.6 1.6 grad_mix.3.refs_4_.refs_7_
  159.4 5.8 %reduce-scatter.5.cloned.1.call-done = bf16[144,1792]{1,0:T(8,128)(2,1)} async-done(((bf16[1152,1792]{1,0:T(8,128)(2,1)}), bf16[144,1792]{1,0:T(8,128)(2,1)}) %reduce-scatter.5.cloned.1.call-update) | async-done | bytes 516112 | tf_op jit(solution)/shard_map/reduce_scatter | solution.py:1266
  165.2 1.8 collective-permute-start.28
  167.0 49.0 %reduce-scatter.3.cloned.1.call-done = bf16[144,1792]{1,0:T(8,128)(2,1)} async-done(((bf16[1152,1792]{1,0:T(8,128)(2,1)}), bf16[144,1792]{1,0:T(8,128)(2,1)}) %reduce-scatter.3.cloned.1.call-update) | async-done | bytes 516112 | tf_op jit(solution)/shard_map/reduce_scatter | solution.py:1266
  216.1 1.5 collective-permute-start.29
  217.5 1.1 broadcast_select_fusion.1
  218.7 1.4 collective-permute-done.29
  220.1 1.0 pad_maximum_fusion
  221.2 1.5 collective-permute-start.22
  223.3 5.5 %collective-permute-done.22.refs_4_ = bf16[128,768]{1,0:T(8,128)(2,1)S(1)} collective-permute-done((bf16[128,768]{1,0:T(8,128)(2,1)S(1)}, bf16[128,768]{1,0:T(8,128)(2,1)S(1)}, u32[]{:S(2)}, u32[]{:S(2)}) %collective-permute-start.22) | collective-permute-done | bytes 196640 | tf_op jit(solution)/shard_map/ppermute | solution.py:1146
  228.8 2.6 input_grad0.1
  231.5 0.6 collective-permute-start.24
  232.1 1.1 select_bitcast_fusion
  233.3 2.3 output1.1
  235.6 1.0 select_bitcast_fusion.1
  237.2 1.5 collective-permute-start.25
  238.6 6.4 %collective-permute-done.25 = f32[102,256]{1,0:T(8,128)S(1)} collective-permute-done((f32[102,256]{1,0:T(8,128)S(1)}, f32[102,256]{1,0:T(8,128)S(1)}, u32[]{:S(2)}, u32[]{:S(2)}) %collective-permute-start.25) | collective-permute-done | bytes 104480 | tf_op jit(solution)/shard_map/ppermute | solution.py:1310
  245.1 0.8 maximum_select_fusion.1
  245.9 6.7 %collective-permute-done.26 = f32[102,256]{1,0:T(8,128)S(1)} collective-permute-done((f32[102,256]{1,0:T(8,128)S(1)}, f32[102,256]{1,0:T(8,128)S(1)}, u32[]{:S(2)}, u32[]{:S(2)}) %collective-permute-start.26) | collective-permute-done | bytes 104480 | tf_op jit(solution)/shard_map/ppermute | solution.py:1310
  252.6 2.0 collective-permute-start.27
  254.6 0.9 maximum_select_fusion
  255.5 7.2 %collective-permute-done.27 = f32[102,256]{1,0:T(8,128)S(1)} collective-permute-done((f32[102,256]{1,0:T(8,128)S(1)}, f32[102,256]{1,0:T(8,128)S(1)}, u32[]{:S(2)}, u32[]{:S(2)}) %collective-permute-start.27) | collective-permute-done | bytes 104480 | tf_op jit(solution)/shard_map/ppermute | solution.py:1310
  263.3 0.6 copy.47
  264.2 0.7 copy.52
  264.9 0.6 copy.50
  265.6 0.6 copy.49
  266.1 0.6 copy.51
  266.7 0.6 copy.48
  267.4 0.6 maximum_bitcast_fusion.1
  268.0 44.7 %all-gather.2.cloned.1.call-done.refs_0_ = bf16[1152,3584]{1,0:T(8,128)(2,1)} async-done(((bf16[144,3584]{1,0:T(8,128)(2,1)}), bf16[1152,3584]{1,0:T(8,128)(2,1)}) %all-gather.2.cloned.1.call-update) | async-done | bytes 8257552 | tf_op jit(solution)/shard_map/all_gather | solution.py:1292
  312.7 7.8 %final.1 = (f32[768,2,1024]{2,1,0:T(2,128)}, f32[1024,768]{1,0:T(8,128)}, f32[768,4,384]{2,1,0:T(4,128)}, f32[384,768]{1,0:T(8,128)}, f32[384,256]{1,0:T(8,128)}, /*index=5*/f32[384,256]{1,0:T(8,128)}) custom-call(bf16[1152,3584]{1,0:T(8,128)(2,1)} %all-gather.2.cloned.1.call-done.refs_0_), custom_call_target="tpu_custom_call" | custom-call | tf_op jit(solution)/shard_map/final/pallas_call | solution.py:1109
  (114 shorter events, 6.9 us)
Async XLA Ops:
  7.2 3.0 copy-start.2
  7.2 3.0 copy-start.3
  7.2 3.0 copy-start.7
  7.2 3.0 copy-start.8
  7.2 3.0 copy-start.10
  7.2 3.0 copy-start.9
  7.2 3.0 copy-start.11
  7.3 3.0 copy-start.6
  7.3 3.0 copy-start.12
  7.3 157.9 %reduce-scatter.5.cloned.1.call-start = ((), (), s32[]{:S(2)}) async-start(), calls=%async_computation.3 | async-start | bytes 4644864 | tf_op jit(solution)/shard_map/reduce_scatter | solution.py:1266
  7.3 2.8 copy-start.20
  7.3 4.0 %copy-start.21 = (bf16[1,768,2,1024]{3,2,1,0:T(2,128)(2,1)S(1)}, bf16[1,768,2,1024]{3,2,1,0:T(2,128)(2,1)}, u32[]{:S(2)}) copy-start(bf16[1,768,2,1024]{3,2,1,0:T(2,128)(2,1)} %param.29) | copy-start | bytes 9437188
  9.6 4.5 %copy-start.13 = (bf16[96,8,4,384]{3,1,2,0:T(8,128)(2,1)}, bf16[96,8,4,384]{3,1,2,0:T(8,128)(2,1)S(1)}, u32[]{:S(2)}) copy-start(bf16[96,8,4,384]{3,1,2,0:T(8,128)(2,1)S(1)} %copy.53) | copy-start | bytes 7077892
  9.6 6.2 %collective-permute-start.1 = (bf16[768,1536]{1,0:T(8,128)(2,1)S(1)}, bf16[768,1536]{1,0:T(8,128)(2,1)S(1)}, u32[]{:S(2)}, u32[]{:S(2)}) collective-permute-start(bf16[768,1536]{1,0:T(8,128)(2,1)S(1)} %bitcast.82), channel_id=1, source_target_pairs={{0,16},{16,0},{1,17},{17,1},{2,18},{18,2},{3,19},{19,3},{4,20},{20... | collective-permute-start | bytes 7077896 | tf_op jit(solution)/shard_map/ppermute | solution.py:1146
  10.1 5.6 %collective-permute-start.4 = (bf16[384,768]{1,0:T(8,128)(2,1)S(1)}, bf16[384,768]{1,0:T(8,128)(2,1)S(1)}, u32[]{:S(2)}, u32[]{:S(2)}) collective-permute-start(bf16[384,768]{1,0:T(8,128)(2,1)S(1)} %bitcast.95), channel_id=1, source_target_pairs={{0,16},{16,0},{1,17},{17,1},{2,18},{18,2},{3,19},{19,3},{4,20},{20... | collective-permute-start | bytes 1769480 | tf_op jit(solution)/shard_map/ppermute | solution.py:1146
  10.3 3.7 %copy-start = (bf16[12,64,256]{2,1,0:T(8,128)(2,1)}, bf16[12,64,256]{2,1,0:T(8,128)(2,1)S(1)}, u32[]{:S(2)}) copy-start(bf16[12,64,256]{2,1,0:T(8,128)(2,1)S(1)} %get-tuple-element.90.refs_8_.refs_10_.refs_25_) | copy-start | bytes 1179652
  10.3 3.7 %copy-start.1 = (f32[4,1536]{1,0:T(4,128)}, f32[4,1536]{1,0:T(4,128)S(1)}, u32[]{:S(2)}) copy-start(f32[4,1536]{1,0:T(4,128)S(1)} %get-tuple-element.88.refs_2_.refs_3_.refs_4_.refs_5_.refs_19_) | copy-start | bytes 73732
  10.4 3.7 %copy-start.4 = (bf16[16,768]{1,0:T(8,128)(2,1)}, bf16[16,768]{1,0:T(8,128)(2,1)S(1)}, u32[]{:S(2)}) copy-start(bf16[16,768]{1,0:T(8,128)(2,1)S(1)} %get-tuple-element.89.refs_6_.refs_8_.refs_23_) | copy-start | bytes 73732
  10.4 5.4 %collective-permute-start.3 = (bf16[12,64,256]{2,1,0:T(8,128)(2,1)S(1)}, bf16[12,64,256]{2,1,0:T(8,128)(2,1)S(1)}, u32[]{:S(2)}, u32[]{:S(2)}) collective-permute-start(bf16[12,64,256]{2,1,0:T(8,128)(2,1)S(1)} %get-tuple-element.90.refs_8_.refs_10_.refs_25_), channel_id=1, source_target_pairs={{0,16},{16,0},{1,17},{17,1},{2,18},{18,2},{3,19},{19,3},{4,20},{20... | collective-permute-start | bytes 1179656 | tf_op jit(solution)/shard_map/ppermute | solution.py:1146
  10.9 4.8 %collective-permute-start = (f32[4,1536]{1,0:T(4,128)S(1)}, f32[4,1536]{1,0:T(4,128)S(1)}, u32[]{:S(2)}, u32[]{:S(2)}) collective-permute-start(f32[4,1536]{1,0:T(4,128)S(1)} %get-tuple-element.88.refs_2_.refs_3_.refs_4_.refs_5_.refs_19_), channel_id=1, source_target_pairs={{0,16},{16,0},{1,17},{17,1},{2,18},{18,2},{3,19},{19,3},{4,20},{20... | collective-permute-start | bytes 73736 | tf_op jit(solution)/shard_map/ppermute | solution.py:1146
  10.9 4.8 %collective-permute-start.2 = (bf16[16,768]{1,0:T(8,128)(2,1)S(1)}, bf16[16,768]{1,0:T(8,128)(2,1)S(1)}, u32[]{:S(2)}, u32[]{:S(2)}) collective-permute-start(bf16[16,768]{1,0:T(8,128)(2,1)S(1)} %get-tuple-element.89.refs_6_.refs_8_.refs_23_), channel_id=1, source_target_pairs={{0,16},{16,0},{1,17},{17,1},{2,18},{18,2},{3,19},{19,3},{4,20},{20... | collective-permute-start | bytes 73736 | tf_op jit(solution)/shard_map/ppermute | solution.py:1146
  15.7 2.5 copy-start.22
  15.7 2.4 copy-start.23
  15.7 0.7 copy-start.19
  15.7 1.0 copy-start.16
  16.7 1.5 copy-start.14
  18.2 1.4 copy-start.17
  18.2 1.8 copy-start.5
  18.2 27.6 %collective-permute-start.6 = (bf16[768,2048]{1,0:T(8,128)(2,1)}, bf16[768,2048]{1,0:T(8,128)(2,1)S(1)}, u32[]{:S(2)}, u32[]{:S(2)}) collective-permute-start(bf16[768,2048]{1,0:T(8,128)(2,1)} %gate.1.refs_5_.refs_7_.refs_11_), channel_id=1, source_target_pairs={{0,16},{16,0},{1,17},{17,1},{2,18},{18,2},{3,19},{19,3},{4,20},{20... | collective-permute-start | bytes 9437192 | tf_op jit(solution)/shard_map/ppermute | solution.py:1146
  19.6 20.8 %collective-permute-start.7 = (bf16[1024,768]{1,0:T(8,128)(2,1)S(1)}, bf16[1024,768]{1,0:T(8,128)(2,1)S(1)}, u32[]{:S(2)}, u32[]{:S(2)}) collective-permute-start(bf16[1024,768]{1,0:T(8,128)(2,1)S(1)} %bitcast.90), channel_id=1, source_target_pairs={{0,16},{16,0},{1,17},{17,1},{2,18},{18,2},{3,19},{19,3},{4,20},{20... | collective-permute-start | bytes 4718600 | tf_op jit(solution)/shard_map/ppermute | solution.py:1146
  37.7 8.1 %collective-permute-start.5 = (bf16[128,768]{1,0:T(8,128)(2,1)S(1)}, bf16[128,768]{1,0:T(8,128)(2,1)S(1)}, u32[]{:S(2)}, u32[]{:S(2)}) collective-permute-start(bf16[128,768]{1,0:T(8,128)(2,1)S(1)} %get-tuple-element.92.refs_1_), channel_id=1, source_target_pairs={{0,1},{1,0},{2,3},{3,2},{4,5},{5,4},{6,7},{7,6},{8,9},{9,8},{10,11... | collective-permute-start | bytes 589832 | tf_op jit(solution)/shard_map/ppermute | solution.py:1146
  40.4 5.4 %copy-start.18 = (bf16[1024,768]{1,0:T(8,128)(2,1)}, bf16[1024,768]{1,0:T(8,128)(2,1)S(1)}, u32[]{:S(2)}) copy-start(bf16[1024,768]{1,0:T(8,128)(2,1)S(1)} %collective-permute-done.7.refs_8_.refs_10_.refs_14_) | copy-start | bytes 4718596
  45.8 1.7 copy-start.15
  51.7 6.7 %collective-permute-start.8 = (bf16[128,768]{1,0:T(8,128)(2,1)S(1)}, bf16[128,768]{1,0:T(8,128)(2,1)S(1)}, u32[]{:S(2)}, u32[]{:S(2)}) collective-permute-start(bf16[128,768]{1,0:T(8,128)(2,1)S(1)} %get-tuple-element.94.refs_2_), channel_id=1, source_target_pairs={{0,1},{1,0},{2,3},{3,2},{4,5},{5,4},{6,7},{7,6},{8,9},{9,8},{10,11... | collective-permute-start | bytes 589832 | tf_op jit(solution)/shard_map/ppermute | solution.py:1146
  73.8 5.8 %collective-permute-start.9 = (bf16[128,768]{1,0:T(8,128)(2,1)S(1)}, bf16[128,768]{1,0:T(8,128)(2,1)S(1)}, u32[]{:S(2)}, u32[]{:S(2)}) collective-permute-start(bf16[128,768]{1,0:T(8,128)(2,1)S(1)} %get-tuple-element.97.refs_3_), channel_id=1, source_target_pairs={{0,1},{1,0},{2,3},{3,2},{4,5},{5,4},{6,7},{7,6},{8,9},{9,8},{10,11... | collective-permute-start | bytes 589832 | tf_op jit(solution)/shard_map/ppermute | solution.py:1146
  85.4 2.4 collective-permute-start.13
  85.5 7.4 %collective-permute-start.11 = (bf16[128,768]{1,0:T(8,128)(2,1)S(1)}, bf16[128,768]{1,0:T(8,128)(2,1)S(1)}, u32[]{:S(2)}, u32[]{:S(2)}) collective-permute-start(bf16[128,768]{1,0:T(8,128)(2,1)S(1)} %get-tuple-element.100.refs_1_), channel_id=1, source_target_pairs={{0,1},{1,0},{2,3},{3,2},{4,5},{5,4},{6,7},{7,6},{8,9},{9,8},{10,11... | collective-permute-start | bytes 589832 | tf_op jit(solution)/shard_map/ppermute | solution.py:1146
  87.0 5.8 %collective-permute-start.12 = (f32[4,16]{1,0:T(4,128)S(1)}, f32[4,16]{1,0:T(4,128)S(1)}, u32[]{:S(2)}, u32[]{:S(2)}) collective-permute-start(f32[4,16]{1,0:T(4,128)S(1)} %pad_maximum_fusion.2.refs_7_), channel_id=1, source_target_pairs={{0,1},{1,0},{2,3},{3,2},{4,5},{5,4},{6,7},{7,6},{8,9},{9,8},{10,11... | collective-permute-start | bytes 776 | tf_op jit(solution)/shard_map/ppermute | solution.py:1146
  111.7 2.6 collective-permute-start.15
  111.8 2.6 collective-permute-start.16
  116.0 100.1 %reduce-scatter.3.cloned.1.call-start = ((), (), s32[]{:S(2)}) async-start(), calls=%async_computation.2 | async-start | bytes 4644864 | tf_op jit(solution)/shard_map/reduce_scatter | solution.py:1266
  116.0 7.0 %collective-permute-start.14 = (bf16[128,768]{1,0:T(8,128)(2,1)S(1)}, bf16[128,768]{1,0:T(8,128)(2,1)S(1)}, u32[]{:S(2)}, u32[]{:S(2)}) collective-permute-start(bf16[128,768]{1,0:T(8,128)(2,1)S(1)} %get-tuple-element.119.refs_3_), channel_id=1, source_target_pairs={{0,1},{1,0},{2,3},{3,2},{4,5},{5,4},{6,7},{7,6},{8,9},{9,8},{10,11... | collective-permute-start | bytes 589832 | tf_op jit(solution)/shard_map/ppermute | solution.py:1146
  129.1 2.4 collective-permute-start.17
  129.2 7.3 %collective-permute-start.18 = (bf16[128,768]{1,0:T(8,128)(2,1)S(1)}, bf16[128,768]{1,0:T(8,128)(2,1)S(1)}, u32[]{:S(2)}, u32[]{:S(2)}) collective-permute-start(bf16[128,768]{1,0:T(8,128)(2,1)S(1)} %get-tuple-element.129.refs_1_), channel_id=1, source_target_pairs={{0,1},{1,0},{2,3},{3,2},{4,5},{5,4},{6,7},{7,6},{8,9},{9,8},{10,11... | collective-permute-start | bytes 589832 | tf_op jit(solution)/shard_map/ppermute | solution.py:1146
  155.0 2.6 collective-permute-start.19
  155.2 2.4 collective-permute-start.20
  159.3 153.4 %all-gather.2.cloned.1.call-start = ((), (), s32[]{:S(2)}) async-start(), calls=%async_computation.4 | async-start | bytes 9289728 | tf_op jit(solution)/shard_map/all_gather | solution.py:1292
  165.2 52.4 %collective-permute-start.28 = (bf16[144,1792]{1,0:T(8,128)(2,1)}, bf16[144,1792]{1,0:T(8,128)(2,1)S(1)}, u32[]{:S(2)}, u32[]{:S(2)}) collective-permute-start(bf16[144,1792]{1,0:T(8,128)(2,1)} %reduce-scatter.5.cloned.1.call-done), channel_id=1, source_target_pairs={{0,16},{1,17},{2,18},{3,19},{4,20},{5,21},{6,22},{7,23},{8,24},{9,... | collective-permute-start | bytes 1548296 | tf_op jit(solution)/shard_map/ppermute | solution.py:1290
  216.1 4.0 %collective-permute-start.29 = (bf16[144,1792]{1,0:T(8,128)(2,1)}, bf16[144,1792]{1,0:T(8,128)(2,1)S(1)}, u32[]{:S(2)}, u32[]{:S(2)}) collective-permute-start(bf16[144,1792]{1,0:T(8,128)(2,1)} %reduce-scatter.3.cloned.1.call-done), channel_id=1, source_target_pairs={{16,0},{17,1},{18,2},{19,3},{20,4},{21,5},{22,6},{23,7},{24,8},{25... | collective-permute-start | bytes 1548296 | tf_op jit(solution)/shard_map/ppermute | solution.py:1291
  221.2 10.9 %copy-start.24 = (f32[128,768]{1,0:T(8,128)S(1)}, f32[128,768]{1,0:T(8,128)}, u32[]{:S(2)}) copy-start(f32[128,768]{1,0:T(8,128)} %get-tuple-element.149) | copy-start | bytes 1179652
  221.2 7.6 %collective-permute-start.22 = (bf16[128,768]{1,0:T(8,128)(2,1)S(1)}, bf16[128,768]{1,0:T(8,128)(2,1)S(1)}, u32[]{:S(2)}, u32[]{:S(2)}) collective-permute-start(bf16[128,768]{1,0:T(8,128)(2,1)S(1)} %get-tuple-element.147.refs_3_), channel_id=1, source_target_pairs={{0,1},{1,0},{2,3},{3,2},{4,5},{5,4},{6,7},{7,6},{8,9},{9,8},{10,11... | collective-permute-start | bytes 589832 | tf_op jit(solution)/shard_map/ppermute | solution.py:1146
  222.7 10.6 %collective-permute-start.10 = (bf16[128,768]{1,0:T(8,128)(2,1)S(1)}, bf16[128,768]{1,0:T(8,128)(2,1)S(1)}, u32[]{:S(2)}, u32[]{:S(2)}) collective-permute-start(bf16[128,768]{1,0:T(8,128)(2,1)S(1)} %get-tuple-element.99.refs_2_), channel_id=1, source_target_pairs={{0,1},{1,0},{2,3},{3,2},{4,5},{5,4},{6,7},{7,6},{8,9},{9,8},{10,11... | collective-permute-start | bytes 589832 | tf_op jit(solution)/shard_map/ppermute | solution.py:1146
  231.5 5.6 %collective-permute-start.24 = (f32[102,256]{1,0:T(8,128)S(1)}, f32[102,256]{1,0:T(8,128)S(1)}, u32[]{:S(2)}, u32[]{:S(2)}) collective-permute-start(f32[102,256]{1,0:T(8,128)S(1)} %pad_maximum_fusion.1), channel_id=1, source_target_pairs={{0,16},{16,0},{1,17},{17,1},{2,18},{18,2},{3,19},{19,3},{4,20},{20... | collective-permute-start | bytes 313352 | tf_op jit(solution)/shard_map/ppermute | solution.py:1146
  232.1 3.5 %copy-start.25 = (bf16[128,768]{1,0:T(8,128)(2,1)S(1)}, bf16[128,768]{1,0:T(8,128)(2,1)}, u32[]{:S(2)}) copy-start(bf16[128,768]{1,0:T(8,128)(2,1)} %get-tuple-element.95) | copy-start | bytes 589828
  233.2 21.4 %collective-permute-start.23 = (f32[128,768]{1,0:T(8,128)S(1)}, f32[128,768]{1,0:T(8,128)S(1)}, u32[]{:S(2)}, u32[]{:S(2)}) collective-permute-start(f32[128,768]{1,0:T(8,128)S(1)} %get-tuple-element.209), channel_id=1, source_target_pairs={{0,16},{16,0},{1,17},{17,1},{2,18},{18,2},{3,19},{19,3},{4,20},{20... | collective-permute-start | bytes 1179656 | tf_op jit(solution)/shard_map/ppermute | solution.py:1146
  236.6 8.5 %collective-permute-start.21 = (bf16[128,768]{1,0:T(8,128)(2,1)S(1)}, bf16[128,768]{1,0:T(8,128)(2,1)S(1)}, u32[]{:S(2)}, u32[]{:S(2)}) collective-permute-start(bf16[128,768]{1,0:T(8,128)(2,1)S(1)} %get-tuple-element.211), channel_id=1, source_target_pairs={{0,16},{16,0},{1,17},{17,1},{2,18},{18,2},{3,19},{19,3},{4,20},{20... | collective-permute-start | bytes 589832 | tf_op jit(solution)/shard_map/ppermute | solution.py:1146
  237.2 7.8 %collective-permute-start.25 = (f32[102,256]{1,0:T(8,128)S(1)}, f32[102,256]{1,0:T(8,128)S(1)}, u32[]{:S(2)}, u32[]{:S(2)}) collective-permute-start(f32[102,256]{1,0:T(8,128)S(1)} %fusion.1), channel_id=1, source_target_pairs={{0,2},{2,0},{4,6},{6,4},{8,10},{10,8},{12,14},{14,12},{1,3},{3,1},... | collective-permute-start | bytes 313352 | tf_op jit(solution)/shard_map/ppermute | solution.py:1310
  245.0 7.6 %collective-permute-start.26 = (f32[102,256]{1,0:T(8,128)S(1)}, f32[102,256]{1,0:T(8,128)S(1)}, u32[]{:S(2)}, u32[]{:S(2)}) collective-permute-start(f32[102,256]{1,0:T(8,128)S(1)} %add.17), channel_id=1, source_target_pairs={{0,4},{2,6},{4,0},{6,2},{8,12},{10,14},{12,8},{14,10},{1,5},{3,7},... | collective-permute-start | bytes 313352 | tf_op jit(solution)/shard_map/ppermute | solution.py:1310
  252.6 10.1 %collective-permute-start.27 = (f32[102,256]{1,0:T(8,128)S(1)}, f32[102,256]{1,0:T(8,128)S(1)}, u32[]{:S(2)}, u32[]{:S(2)}) collective-permute-start(f32[102,256]{1,0:T(8,128)S(1)} %add.18), channel_id=1, source_target_pairs={{0,8},{2,10},{4,12},{6,14},{8,0},{10,2},{12,4},{14,6},{1,9},{3,11}... | collective-permute-start | bytes 313352 | tf_op jit(solution)/shard_map/ppermute | solution.py:1310
Sparse Core Ops, SparseCore 0:
  116.1 49.0 reduce-scatter.4
  168.2 47.8 reduce-scatter.2
  221.3 91.3 all-gather.1
